TPU v7x, 32 devices: a whole 2x2x4 slice. The times are simulated.
32 devices in a mesh: groups: 2 (over x), angle: 8 (over z, y), tile: 2 (over core).
Axes of the slice: x: 2, y: 2, z: 4, core: 2. Of those that a mesh axis runs over, the one named last changes fastest.
Arguments:
- intensity: float32 [128, 128, 2048], P(('groups', 'angle', 'tile')), parts along dimension 0, may hold values from 0.2 to 1
- counts: int32 [16], P('groups'), parts along dimension 0, may hold values from 1 to 32, 128 in all
- segment_ids: int32 [64, 64], replicated, may hold values from 0 to 15
- tile_ids: int32 [64, 64], replicated, may hold values from 0 to 15
- block_order: int32 [128], P('groups'), parts along dimension 0, may hold values from 0 to 63, each once
- tiles: bfloat16 [16, 128, 128], replicated, may hold values from -0.0625 to 0.0625
Outputs:
- volume: float32 [16, 32, 64, 128], P(('groups', 'angle'), None, 'tile'), parts along dimension 0
There are 2 independent parts, one for each index of `groups`. A program takes and returns all parts, laid end to end along the dimension named above; an argument that names none is the same for every part. Nothing has to cross between parts.
Inputs may be any that keep to these rules, and one draw needn't show every extreme that they name: Slice group g takes counts[g] consecutive detector rows, groups in order; the counts sum to 128 and the largest is exactly 32. `block_order`: each voxel block appears once.
All inputs are finite; a program needn't handle non-finite values.
Results may differ from a plain program's by a relative error of at most 0.00075.
Values may be sent and summed in bfloat16 or wider, within the bound.
A program may use at most 128 MiB of HBM per device.

v0:
```python
import functools
import math

import jax
import jax.numpy as jnp
import numpy as np
from jax import lax
from jax.experimental import pallas as pl
from jax.experimental.pallas import tpu as pltpu
from jax.sharding import PartitionSpec as P

paganin_alpha = 2.0
link_type = jnp.float16
chunk_total = 4


def split_pair(array):
    high = array.astype(jnp.bfloat16)
    low = (array - high.astype(jnp.float32)).astype(jnp.bfloat16)
    return high, low


def filter_tables(row_total):
    index = np.arange(row_total)
    phase = 2.0 * np.pi * (index[:, None] * index[None, :] % row_total) / row_total
    hartley = (np.cos(phase) + np.sin(phase)) / math.sqrt(row_total)
    high = hartley.astype(np.float32).astype(jnp.bfloat16)
    low = (hartley - high.astype(np.float64)).astype(np.float32).astype(jnp.bfloat16)
    a = 1.0 + paganin_alpha * (4.0 * np.sin(np.pi * index / row_total) ** 2 + 2.0)
    pole = (a - np.sqrt(a * a - 4.0 * paganin_alpha**2)) / (2.0 * paganin_alpha)
    gain = pole / (paganin_alpha * (1.0 - pole * pole))
    forward = np.concatenate([np.concatenate([high, low], 1)] * 2, 0)
    inverse = np.concatenate([np.concatenate([high, high], 1), np.concatenate([low, low], 1)], 0)
    poles = np.stack([pole, gain]).astype(np.float32)
    return forward, inverse, poles


def filter_kernel(x_ref, forward_ref, inverse_ref, pole_ref, out_ref, spectrum, causal):
    edge = out_ref.shape[-1]
    segments = out_ref.shape[1]
    rows = out_ref.shape[2]
    for s in range(segments):
        high, low = split_pair(x_ref[0, :, s * edge : (s + 1) * edge])
        both = jnp.concatenate([high, low], axis=0)
        product = lax.dot_general(
            both, forward_ref[...], (((0,), (0,)), ((), ())), preferred_element_type=jnp.float32
        )
        spectrum[s * edge : (s + 1) * edge, :] = product[:, :rows] + product[:, rows:]
    pole = jnp.broadcast_to(pole_ref[0:1, :], (segments, rows))
    gain = jnp.broadcast_to(pole_ref[1:2, :], (segments, rows))
    zero = jnp.zeros((segments, rows), jnp.float32)

    def column(t):
        return pl.ds(t, segments, stride=edge)

    def warm(t, state):
        ahead, behind = state
        return (
            ahead * pole + spectrum[column(t), :],
            behind * pole + spectrum[column(edge - 1 - t), :],
        )

    ahead, behind = lax.fori_loop(0, edge, warm, (zero, zero), unroll=8)
    ahead = jnp.concatenate([ahead[segments - 1 :], ahead[: segments - 1]], axis=0)
    behind = jnp.concatenate([behind[1:], behind[:1]], axis=0)

    def sweep(t, state):
        ahead, behind = state
        ahead = ahead * pole + spectrum[column(t), :]
        causal[0, column(t), :] = ahead * gain
        back = edge - 1 - t
        behind = behind * pole
        causal[1, column(back), :] = behind * gain
        return ahead, behind + spectrum[column(back), :]

    lax.fori_loop(0, edge, sweep, (ahead, behind), unroll=8)
    for s in range(segments):
        span = slice(s * edge, (s + 1) * edge)
        high, low = split_pair(causal[0, span, :] + causal[1, span, :])
        both = jnp.concatenate([high, low], axis=1)
        product = lax.dot_general(
            inverse_ref[...], both, (((1,), (1,)), ((), ())), preferred_element_type=jnp.float32
        )
        out_ref[0, s] = (-jnp.log(product[:rows] + product[rows:])).astype(jnp.bfloat16)


def paganin_thickness(intensity, edge):
    angles, rows, width = intensity.shape
    forward, inverse, poles = filter_tables(rows)
    segments = width // edge
    whole = lambda *shape: pl.BlockSpec(shape, lambda a: (0,) * len(shape))
    return pl.pallas_call(
        filter_kernel,
        grid=(angles,),
        out_shape=jax.ShapeDtypeStruct((angles, segments, rows, edge), jnp.bfloat16),
        in_specs=[
            pl.BlockSpec((1, rows, width), lambda a: (a, 0, 0)),
            whole(2 * rows, 2 * rows),
            whole(2 * rows, 2 * rows),
            whole(2, rows),
        ],
        out_specs=pl.BlockSpec((1, segments, rows, edge), lambda a: (a, 0, 0, 0)),
        scratch_shapes=[
            pltpu.VMEM((width, rows), jnp.float32),
            pltpu.VMEM((2, width, rows), jnp.float32),
        ],
        compiler_params=pltpu.CompilerParams(vmem_limit_bytes=32 * 2**20),
        name="paganin_filter",
    )(intensity, jnp.asarray(forward), jnp.asarray(inverse), jnp.asarray(poles))


def backproject_kernel(first, seg_ref, tile_ref, order_ref, start_ref, count_ref, *refs):
    *thick_refs, tiles_ref, out_ref, rows_ref = refs
    groups, block_total, capacity, edge = out_ref.shape
    angles, _, rows, _ = thick_refs[0].shape
    rows_ref[rows:, :] = jnp.zeros((rows_ref.shape[0] - rows, edge), jnp.float32)
    slot = lax.broadcasted_iota(jnp.int32, (capacity, edge), 0)

    def one_block(v, _):
        block = order_ref[first + v]
        pieces, maps = [], []
        for source, thick in enumerate(thick_refs):
            for a in range(angles):
                row = source * angles + a
                pieces.append(thick[a, seg_ref[row, block]])
                maps.append(tiles_ref[tile_ref[row, block]])
        rows_ref[:rows, :] = jnp.dot(
            jnp.concatenate(pieces, axis=1),
            jnp.concatenate(maps, axis=0),
            preferred_element_type=jnp.float32,
        )
        for g in range(groups):
            picked = rows_ref[pl.ds(start_ref[g], capacity), :]
            out_ref[g, v] = jnp.where(slot < count_ref[g], picked, 0.0)
        return 0

    lax.fori_loop(0, block_total, one_block, 0)


def backproject(thick, seg_rows, tile_rows, order, starts, counts, tiles, first, blocks, capacity):
    angles, segments, rows, edge = thick[0].shape
    groups = starts.shape[0]
    smem = pl.BlockSpec(memory_space=pltpu.SMEM)
    vmem = pl.BlockSpec(memory_space=pltpu.VMEM)
    flops = 2 * len(thick) * angles * blocks * rows * edge * edge
    return pl.pallas_call(
        functools.partial(backproject_kernel, first),
        out_shape=jax.ShapeDtypeStruct((groups, blocks, capacity, edge), jnp.float32),
        in_specs=[smem] * 5 + [vmem] * (len(thick) + 1),
        out_specs=vmem,
        scratch_shapes=[pltpu.VMEM((rows + capacity, edge), jnp.float32)],
        compiler_params=pltpu.CompilerParams(vmem_limit_bytes=32 * 2**20),
        cost_estimate=pl.CostEstimate(
            flops=flops, bytes_accessed=4 * groups * blocks * capacity * edge, transcendentals=0
        ),
        name="backproject",
    )(seg_rows, tile_rows, order, starts, counts, *thick, tiles)


def butterfly(partial, scale, lead):
    total = partial.shape[0]
    bits = total.bit_length() - 1
    remaining = list(range(bits - 1, -1, -1))
    current = partial.reshape((2,) * bits + partial.shape[1:])
    order = list(range(bits))
    if bits > 1 and lead:
        order[0], order[1] = order[1], order[0]
    for bit in order:
        axis = remaining.index(bit)
        remaining.remove(bit)
        keep = lax.index_in_dim(current, 0, axis, keepdims=False)
        send = lax.index_in_dim(current, 1, axis, keepdims=False)
        pairs = [(i, i ^ (1 << bit)) for i in range(total)]
        came = lax.ppermute((send * scale).astype(link_type), "angle", pairs)
        current = keep + came.astype(jnp.float32) / scale
    return current


def per_device(intensity, counts, segment_ids, tile_ids, block_order, tiles):
    angles, rows, _ = intensity.shape
    edge = tiles.shape[1]
    groups = lax.axis_size("angle")
    cores = lax.axis_size("tile")
    place = lax.axis_index("angle")
    core = lax.axis_index("tile")
    capacity = 2 * rows // groups
    blocks = block_order.shape[0] // cores
    angle_total = segment_ids.shape[0]

    thickness = paganin_thickness(intensity, edge)
    thick, angle_rows = [thickness], [(place * cores + core) * angles]
    for step in range(1, cores):
        pairs = [(i, (i + step) % cores) for i in range(cores)]
        thick.append(lax.ppermute(thickness, "tile", pairs))
        angle_rows.append((place * cores + (core - step) % cores) * angles)

    seg_rows = jnp.concatenate(
        [lax.dynamic_slice_in_dim(segment_ids, row, angles) for row in angle_rows]
    )
    tile_rows = jnp.concatenate(
        [lax.dynamic_slice_in_dim(tile_ids, row, angles) for row in angle_rows]
    )
    order = lax.dynamic_slice_in_dim(block_order, core * blocks, blocks)
    relative = jnp.arange(groups, dtype=jnp.int32)
    member = relative[None, :] == (relative ^ place)[:, None]
    before = relative[None, :] < (relative ^ place)[:, None]
    near_counts = jnp.sum(jnp.where(member, counts[None, :], 0), axis=1)
    near_starts = jnp.sum(jnp.where(before, counts[None, :], 0), axis=1)

    largest = jnp.max(jnp.abs(tiles.astype(jnp.float32)))
    bound = 1.75 * angle_total * edge * jnp.where(largest > 0.0, largest, 1.0)
    scale = 60000.0 / bound

    chunks = math.gcd(chunk_total, blocks)
    per_chunk = blocks // chunks
    finished = []
    for c in range(chunks):
        partial = backproject(
            thick, seg_rows, tile_rows, order, near_starts, near_counts, tiles,
            c * per_chunk, per_chunk, capacity,
        )
        finished.append(butterfly(partial, scale, c % 2))
    volume = jnp.concatenate(finished, axis=0)
    return jnp.swapaxes(volume, 0, 1)[None]


def solution(mesh):
    in_specs = (P(("groups", "angle", "tile"), None, None), P("groups"), P(), P(), P("groups"), P())
    out_specs = P(("groups", "angle"), None, "tile", None)
    return jax.shard_map(
        per_device, mesh=mesh, in_specs=in_specs, out_specs=out_specs, check_vma=False
    )
```

profile of v0, /device:TPU:0, one launch (start us, length us, event | category | flops | bytes accessed | tf_op | source)
XLA Modules:
  0.0 76.3 jit_solution(9257017576263133886)
XLA Ops:
  0.0 2.2 %copy-done.1 = f32[4,128,2048]{2,1,0:T(8,128)S(1)} copy-done((f32[4,128,2048]{2,1,0:T(8,128)S(1)}, f32[4,128,2048]{2,1,0:T(8,128)}, u32[]{:S(2)}) %copy-start.1) | copy-done | bytes 4194328
  2.3 0.9 %copy-done.2 = bf16[256,256]{1,0:T(8,128)(2,1)S(1)} copy-done((bf16[256,256]{1,0:T(8,128)(2,1)S(1)}, bf16[256,256]{1,0:T(8,128)(2,1)}, u32[]{:S(2)}) %copy-start.2) | copy-done | bytes 131096
  3.2 0.9 %copy-done.3 = bf16[256,256]{1,0:T(8,128)(2,1)S(1)} copy-done((bf16[256,256]{1,0:T(8,128)(2,1)S(1)}, bf16[256,256]{1,0:T(8,128)(2,1)}, u32[]{:S(2)}) %copy-start.3) | copy-done | bytes 131096
  4.1 0.7 copy-done.4
  4.7 21.0 %paganin_filter.1.refs_0_ = bf16[4,16,128,128]{3,2,1,0:T(8,128)(2,1)S(1)} custom-call(f32[4,128,2048]{2,1,0:T(8,128)S(1)} %copy-done.1, bf16[256,256]{1,0:T(8,128)(2,1)S(1)} %copy-done.3, bf16[256,256]{1,0:T(8,128)(2,1)S(1)} %copy-done.2, f32[2,128]{1,0:T(2,128)S(1)} %copy-done.4), custom_call_target="tpu_custom_call" | custom-call | tf_op jit(solution)/shard_map/paganin_filter/pallas_call | solution.py:92
  25.8 0.5 collective-permute-start
  26.3 0.7 abs_reduce_fusion
  28.4 0.8 %constant_dynamic-slice_fusion.1 = (s32[4,64]{1,0:T(4,128)S(1)}, s32[4,64]{1,0:T(4,128)S(1)}, s32[4,64]{1,0:T(4,128)S(1)}, s32[4,64]{1,0:T(4,128)S(1)}) fusion(s32[64,64]{1,0:T(8,128)} %param.12, s32[]{:T(128)S(6)} %select_n.29, s32[]{:T(128)S(6)} %select_n.31, s32[64,64]{1,0:T(8,128)} %param.11), kind=kLoop, calls=%fused_computation.69 | loop fusion | bytes 8200 | tf_op jit(solution)/shard_map/dynamic_slice | solution.py:201
  29.4 0.8 %collective-permute-done.refs_1_ = bf16[4,16,128,128]{3,2,1,0:T(8,128)(2,1)} collective-permute-done((bf16[4,16,128,128]{3,2,1,0:T(8,128)(2,1)S(1)}, bf16[4,16,128,128]{3,2,1,0:T(8,128)(2,1)}, u32[]{:S(2)}, u32[]{:S(2)}) %collective-permute-start) | collective-permute-done | bytes 2097184 | tf_op jit(solution)/shard_map/ppermute | solution.py:194
  30.2 3.5 %backproject.7 = f32[8,8,32,128]{3,2,1,0:T(8,128)S(1)} custom-call(s32[8,64]{1,0:T(8,128)S(1)} %pad_add_fusion.seg_ref, s32[8,64]{1,0:T(8,128)S(1)} %pad_add_fusion.1.tile_ref, s32[32]{0:T(128)S(1)} %dynamic_slice.19.order_ref, s32[8]{0:T(128)S(1)} %get-tuple-element.6.start_ref, s32[8]{0:T(128)S(1)} %get-tuple-element.5.count_ref, ...), custom_call_target="tpu_custom_call" | custom-call | flops 268435456 | bytes 1048576 | tf_op jit(solution)/shard_map/backproject/pallas_call | solution.py:146
  34.1 3.0 %collective-permute-start.10 = (f16[2,2,8,32,128]{4,2,3,0,1:T(8,128)(2,1)S(1)}, f16[2,2,8,32,128]{4,2,3,0,1:T(8,128)(2,1)S(1)}, u32[]{:S(2)}, u32[]{:S(2)}) collective-permute-start(f16[2,2,8,32,128]{4,2,3,0,1:T(8,128)(2,1)S(1)} %fusion.11), channel_id=1, source_target_pairs={{0,4},{2,6},{4,0},{6,2},{8,12},{10,14},{12,8},{14,10},{1,5},{3,7},... | collective-permute-start | bytes 786440 | tf_op jit(solution)/shard_map/ppermute | solution.py:174
  37.1 3.5 %backproject.6 = f32[8,8,32,128]{3,2,1,0:T(8,128)S(1)} custom-call(s32[8,64]{1,0:T(8,128)S(1)} %pad_add_fusion.seg_ref, s32[8,64]{1,0:T(8,128)S(1)} %pad_add_fusion.1.tile_ref, s32[32]{0:T(128)S(1)} %dynamic_slice.19.order_ref, s32[8]{0:T(128)S(1)} %get-tuple-element.6.start_ref, s32[8]{0:T(128)S(1)} %get-tuple-element.5.count_ref, ...), custom_call_target="tpu_custom_call" | custom-call | flops 268435456 | bytes 1048576 | tf_op jit(solution)/shard_map/backproject/pallas_call | solution.py:146
  41.0 1.6 %collective-permute-start.7 = (f16[2,2,8,32,128]{4,2,3,0,1:T(8,128)(2,1)S(1)}, f16[2,2,8,32,128]{4,2,3,0,1:T(8,128)(2,1)S(1)}, u32[]{:S(2)}, u32[]{:S(2)}) collective-permute-start(f16[2,2,8,32,128]{4,2,3,0,1:T(8,128)(2,1)S(1)} %fusion.10), channel_id=1, source_target_pairs={{0,2},{2,0},{4,6},{6,4},{8,10},{10,8},{12,14},{14,12},{1,3},{3,1},... | collective-permute-start | bytes 786440 | tf_op jit(solution)/shard_map/ppermute | solution.py:174
  42.6 3.5 %backproject.5 = f32[8,8,32,128]{3,2,1,0:T(8,128)S(1)} custom-call(s32[8,64]{1,0:T(8,128)S(1)} %pad_add_fusion.seg_ref, s32[8,64]{1,0:T(8,128)S(1)} %pad_add_fusion.1.tile_ref, s32[32]{0:T(128)S(1)} %dynamic_slice.19.order_ref, s32[8]{0:T(128)S(1)} %get-tuple-element.6.start_ref, s32[8]{0:T(128)S(1)} %get-tuple-element.5.count_ref, ...), custom_call_target="tpu_custom_call" | custom-call | flops 268435456 | bytes 1048576 | tf_op jit(solution)/shard_map/backproject/pallas_call | solution.py:146
  46.2 3.5 %backproject.4 = f32[8,8,32,128]{3,2,1,0:T(8,128)S(1)} custom-call(s32[8,64]{1,0:T(8,128)S(1)} %pad_add_fusion.seg_ref, s32[8,64]{1,0:T(8,128)S(1)} %pad_add_fusion.1.tile_ref, s32[32]{0:T(128)S(1)} %dynamic_slice.19.order_ref, s32[8]{0:T(128)S(1)} %get-tuple-element.6.start_ref, s32[8]{0:T(128)S(1)} %get-tuple-element.5.count_ref, ...), custom_call_target="tpu_custom_call" | custom-call | flops 268435456 | bytes 1048576 | tf_op jit(solution)/shard_map/backproject/pallas_call | solution.py:146
  50.1 0.6 collective-permute-start.1
  51.1 0.3 fusion.1
  51.4 2.0 %collective-permute-start.11 = (f16[2,8,32,128]{3,1,2,0:T(8,128)(2,1)S(1)}, f16[2,8,32,128]{3,1,2,0:T(8,128)(2,1)S(1)}, u32[]{:S(2)}, u32[]{:S(2)}) collective-permute-start(f16[2,8,32,128]{3,1,2,0:T(8,128)(2,1)S(1)} %fusion.23), channel_id=1, source_target_pairs={{0,2},{2,0},{4,6},{6,4},{8,10},{10,8},{12,14},{14,12},{1,3},{3,1},... | collective-permute-start | bytes 393224 | tf_op jit(solution)/shard_map/ppermute | solution.py:174
  53.4 0.3 fusion.3
  53.8 1.6 %collective-permute-start.8 = (f16[2,8,32,128]{3,1,2,0:T(8,128)(2,1)S(1)}, f16[2,8,32,128]{3,1,2,0:T(8,128)(2,1)S(1)}, u32[]{:S(2)}, u32[]{:S(2)}) collective-permute-start(f16[2,8,32,128]{3,1,2,0:T(8,128)(2,1)S(1)} %fusion.22), channel_id=1, source_target_pairs={{0,4},{2,6},{4,0},{6,2},{8,12},{10,14},{12,8},{14,10},{1,5},{3,7},... | collective-permute-start | bytes 393224 | tf_op jit(solution)/shard_map/ppermute | solution.py:174
  55.5 3.9 %collective-permute-done.1 = f16[2,2,8,32,128]{4,2,3,0,1:T(8,128)(2,1)S(1)} collective-permute-done((f16[2,2,8,32,128]{4,2,3,0,1:T(8,128)(2,1)S(1)}, f16[2,2,8,32,128]{4,2,3,0,1:T(8,128)(2,1)S(1)}, u32[]{:S(2)}, u32[]{:S(2)}) %collective-permute-start.1) | collective-permute-done | bytes 262176 | tf_op jit(solution)/shard_map/ppermute | solution.py:174
  59.7 0.5 collective-permute-start.2
  60.3 0.3 fusion.5
  60.7 1.6 %collective-permute-start.5 = (f16[2,8,32,128]{3,1,2,0:T(8,128)(2,1)S(1)}, f16[2,8,32,128]{3,1,2,0:T(8,128)(2,1)S(1)}, u32[]{:S(2)}, u32[]{:S(2)}) collective-permute-start(f16[2,8,32,128]{3,1,2,0:T(8,128)(2,1)S(1)} %fusion.21), channel_id=1, source_target_pairs={{0,2},{2,0},{4,6},{6,4},{8,10},{10,8},{12,14},{14,12},{1,3},{3,1},... | collective-permute-start | bytes 393224 | tf_op jit(solution)/shard_map/ppermute | solution.py:174
  62.3 2.7 %collective-permute-start.12 = (f16[8,32,128]{2,0,1:T(8,128)(2,1)S(1)}, f16[8,32,128]{2,0,1:T(8,128)(2,1)S(1)}, u32[]{:S(2)}, u32[]{:S(2)}) collective-permute-start(f16[8,32,128]{2,0,1:T(8,128)(2,1)S(1)} %fusion.35), channel_id=1, source_target_pairs={{0,8},{2,10},{4,12},{6,14},{8,0},{10,2},{12,4},{14,6},{1,9},{3,11}... | collective-permute-start | bytes 196616 | tf_op jit(solution)/shard_map/ppermute | solution.py:174
  65.1 0.8 %collective-permute-start.9 = (f16[8,32,128]{2,0,1:T(8,128)(2,1)S(1)}, f16[8,32,128]{2,0,1:T(8,128)(2,1)S(1)}, u32[]{:S(2)}, u32[]{:S(2)}) collective-permute-start(f16[8,32,128]{2,0,1:T(8,128)(2,1)S(1)} %fusion.34), channel_id=1, source_target_pairs={{0,8},{2,10},{4,12},{6,14},{8,0},{10,2},{12,4},{14,6},{1,9},{3,11}... | collective-permute-start | bytes 196616 | tf_op jit(solution)/shard_map/ppermute | solution.py:174
  66.0 3.0 %collective-permute-start.3 = (f16[8,32,128]{2,0,1:T(8,128)(2,1)S(1)}, f16[8,32,128]{2,0,1:T(8,128)(2,1)S(1)}, u32[]{:S(2)}, u32[]{:S(2)}) collective-permute-start(f16[8,32,128]{2,0,1:T(8,128)(2,1)S(1)} %fusion.32), channel_id=1, source_target_pairs={{0,8},{2,10},{4,12},{6,14},{8,0},{10,2},{12,4},{14,6},{1,9},{3,11}... | collective-permute-start | bytes 196616 | tf_op jit(solution)/shard_map/ppermute | solution.py:174
  69.2 2.7 %collective-permute-done.12 = f16[8,32,128]{2,0,1:T(8,128)(2,1)S(1)} collective-permute-done((f16[8,32,128]{2,0,1:T(8,128)(2,1)S(1)}, f16[8,32,128]{2,0,1:T(8,128)(2,1)S(1)}, u32[]{:S(2)}, u32[]{:S(2)}) %collective-permute-start.12) | collective-permute-done | bytes 65568 | tf_op jit(solution)/shard_map/ppermute | solution.py:174
  71.9 2.1 %collective-permute-done.9 = f16[8,32,128]{2,0,1:T(8,128)(2,1)S(1)} collective-permute-done((f16[8,32,128]{2,0,1:T(8,128)(2,1)S(1)}, f16[8,32,128]{2,0,1:T(8,128)(2,1)S(1)}, u32[]{:S(2)}, u32[]{:S(2)}) %collective-permute-start.9) | collective-permute-done | bytes 65568 | tf_op jit(solution)/shard_map/ppermute | solution.py:174
  74.0 0.7 collective-permute-done.3
  74.8 0.7 collective-permute-done.6
  75.5 0.8 %maximum_bitcast_fusion = f32[1,32,32,128]{3,2,1,0:T(8,128)} fusion(f32[8,32,128]{2,0,1:T(8,128)S(1)} %fusion.25, f32[8,32,128]{2,0,1:T(8,128)S(1)} %fusion.27, f32[8,32,128]{2,0,1:T(8,128)S(1)} %fusion.29, f32[8,32,128]{2,0,1:T(8,128)S(1)} %fusion.31), kind=kLoop, calls=%fused_computation.1 | loop fusion | flops 393216 | bytes 1048576 | tf_op jit(solution)/shard_map/broadcast_in_dim | solution.py:224
  (49 shorter events, 2.8 us)
Async XLA Ops:
  0.0 26.3 %copy-start = (bf16[16,128,128]{2,1,0:T(8,128)(2,1)S(1)}, bf16[16,128,128]{2,1,0:T(8,128)(2,1)}, u32[]{:S(2)}) copy-start(bf16[16,128,128]{2,1,0:T(8,128)(2,1)} %refs_2_.7) | copy-start | bytes 1572868
  0.0 2.2 %copy-start.1 = (f32[4,128,2048]{2,1,0:T(8,128)S(1)}, f32[4,128,2048]{2,1,0:T(8,128)}, u32[]{:S(2)}) copy-start(f32[4,128,2048]{2,1,0:T(8,128)} %x_ref.1) | copy-start | bytes 12582916
  2.2 0.9 %copy-start.2 = (bf16[256,256]{1,0:T(8,128)(2,1)S(1)}, bf16[256,256]{1,0:T(8,128)(2,1)}, u32[]{:S(2)}) copy-start(bf16[256,256]{1,0:T(8,128)(2,1)} %constant.48.clone.inverse_ref) | copy-start | bytes 393220
  3.2 0.9 %copy-start.3 = (bf16[256,256]{1,0:T(8,128)(2,1)S(1)}, bf16[256,256]{1,0:T(8,128)(2,1)}, u32[]{:S(2)}) copy-start(bf16[256,256]{1,0:T(8,128)(2,1)} %constant.47.clone.forward_ref) | copy-start | bytes 393220
  4.1 0.7 copy-start.4
  4.7 23.6 %copy-start.6 = (s32[64]{0:T(128)S(1)}, s32[64]{0:T(128)}, u32[]{:S(2)}) copy-start(s32[64]{0:T(128)} %param.13) | copy-start | bytes 772
  4.7 24.5 %copy-start.5 = (s32[8]{0:T(128)S(1)}, s32[8]{0:T(128)}, u32[]{:S(2)}) copy-start(s32[8]{0:T(128)} %param.10) | copy-start | bytes 100
  25.8 4.4 %collective-permute-start = (bf16[4,16,128,128]{3,2,1,0:T(8,128)(2,1)S(1)}, bf16[4,16,128,128]{3,2,1,0:T(8,128)(2,1)}, u32[]{:S(2)}, u32[]{:S(2)}) collective-permute-start(bf16[4,16,128,128]{3,2,1,0:T(8,128)(2,1)S(1)} %paganin_filter.1.refs_0_), channel_id=1, source_target_pairs={{0,1},{1,0},{2,3},{3,2},{4,5},{5,4},{6,7},{7,6},{8,9},{9,8},{10,11... | collective-permute-start | bytes 6291464 | tf_op jit(solution)/shard_map/ppermute | solution.py:194
  34.1 17.0 %collective-permute-start.10 = (f16[2,2,8,32,128]{4,2,3,0,1:T(8,128)(2,1)S(1)}, f16[2,2,8,32,128]{4,2,3,0,1:T(8,128)(2,1)S(1)}, u32[]{:S(2)}, u32[]{:S(2)}) collective-permute-start(f16[2,2,8,32,128]{4,2,3,0,1:T(8,128)(2,1)S(1)} %fusion.11), channel_id=1, source_target_pairs={{0,4},{2,6},{4,0},{6,2},{8,12},{10,14},{12,8},{14,10},{1,5},{3,7},... | collective-permute-start | bytes 786440 | tf_op jit(solution)/shard_map/ppermute | solution.py:174
  41.0 12.4 %collective-permute-start.7 = (f16[2,2,8,32,128]{4,2,3,0,1:T(8,128)(2,1)S(1)}, f16[2,2,8,32,128]{4,2,3,0,1:T(8,128)(2,1)S(1)}, u32[]{:S(2)}, u32[]{:S(2)}) collective-permute-start(f16[2,2,8,32,128]{4,2,3,0,1:T(8,128)(2,1)S(1)} %fusion.10), channel_id=1, source_target_pairs={{0,2},{2,0},{4,6},{6,4},{8,10},{10,8},{12,14},{14,12},{1,3},{3,1},... | collective-permute-start | bytes 786440 | tf_op jit(solution)/shard_map/ppermute | solution.py:174
  50.1 9.3 %collective-permute-start.1 = (f16[2,2,8,32,128]{4,2,3,0,1:T(8,128)(2,1)S(1)}, f16[2,2,8,32,128]{4,2,3,0,1:T(8,128)(2,1)S(1)}, u32[]{:S(2)}, u32[]{:S(2)}) collective-permute-start(f16[2,2,8,32,128]{4,2,3,0,1:T(8,128)(2,1)S(1)} %fusion.8), channel_id=1, source_target_pairs={{0,2},{2,0},{4,6},{6,4},{8,10},{10,8},{12,14},{14,12},{1,3},{3,1},... | collective-permute-start | bytes 786440 | tf_op jit(solution)/shard_map/ppermute | solution.py:174
  51.0 9.3 %collective-permute-start.4 = (f16[2,2,8,32,128]{4,2,3,0,1:T(8,128)(2,1)S(1)}, f16[2,2,8,32,128]{4,2,3,0,1:T(8,128)(2,1)S(1)}, u32[]{:S(2)}, u32[]{:S(2)}) collective-permute-start(f16[2,2,8,32,128]{4,2,3,0,1:T(8,128)(2,1)S(1)} %fusion.9), channel_id=1, source_target_pairs={{0,4},{2,6},{4,0},{6,2},{8,12},{10,14},{12,8},{14,10},{1,5},{3,7},... | collective-permute-start | bytes 786440 | tf_op jit(solution)/shard_map/ppermute | solution.py:174
  51.4 10.8 %collective-permute-start.11 = (f16[2,8,32,128]{3,1,2,0:T(8,128)(2,1)S(1)}, f16[2,8,32,128]{3,1,2,0:T(8,128)(2,1)S(1)}, u32[]{:S(2)}, u32[]{:S(2)}) collective-permute-start(f16[2,8,32,128]{3,1,2,0:T(8,128)(2,1)S(1)} %fusion.23), channel_id=1, source_target_pairs={{0,2},{2,0},{4,6},{6,4},{8,10},{10,8},{12,14},{14,12},{1,3},{3,1},... | collective-permute-start | bytes 393224 | tf_op jit(solution)/shard_map/ppermute | solution.py:174
  53.8 11.2 %collective-permute-start.8 = (f16[2,8,32,128]{3,1,2,0:T(8,128)(2,1)S(1)}, f16[2,8,32,128]{3,1,2,0:T(8,128)(2,1)S(1)}, u32[]{:S(2)}, u32[]{:S(2)}) collective-permute-start(f16[2,8,32,128]{3,1,2,0:T(8,128)(2,1)S(1)} %fusion.22), channel_id=1, source_target_pairs={{0,4},{2,6},{4,0},{6,2},{8,12},{10,14},{12,8},{14,10},{1,5},{3,7},... | collective-permute-start | bytes 393224 | tf_op jit(solution)/shard_map/ppermute | solution.py:174
  59.7 6.2 %collective-permute-start.2 = (f16[2,8,32,128]{3,1,2,0:T(8,128)(2,1)S(1)}, f16[2,8,32,128]{3,1,2,0:T(8,128)(2,1)S(1)}, u32[]{:S(2)}, u32[]{:S(2)}) collective-permute-start(f16[2,8,32,128]{3,1,2,0:T(8,128)(2,1)S(1)} %fusion.20), channel_id=1, source_target_pairs={{0,4},{2,6},{4,0},{6,2},{8,12},{10,14},{12,8},{14,10},{1,5},{3,7},... | collective-permute-start | bytes 393224 | tf_op jit(solution)/shard_map/ppermute | solution.py:174
  60.7 8.4 %collective-permute-start.5 = (f16[2,8,32,128]{3,1,2,0:T(8,128)(2,1)S(1)}, f16[2,8,32,128]{3,1,2,0:T(8,128)(2,1)S(1)}, u32[]{:S(2)}, u32[]{:S(2)}) collective-permute-start(f16[2,8,32,128]{3,1,2,0:T(8,128)(2,1)S(1)} %fusion.21), channel_id=1, source_target_pairs={{0,2},{2,0},{4,6},{6,4},{8,10},{10,8},{12,14},{14,12},{1,3},{3,1},... | collective-permute-start | bytes 393224 | tf_op jit(solution)/shard_map/ppermute | solution.py:174
  62.3 9.6 %collective-permute-start.12 = (f16[8,32,128]{2,0,1:T(8,128)(2,1)S(1)}, f16[8,32,128]{2,0,1:T(8,128)(2,1)S(1)}, u32[]{:S(2)}, u32[]{:S(2)}) collective-permute-start(f16[8,32,128]{2,0,1:T(8,128)(2,1)S(1)} %fusion.35), channel_id=1, source_target_pairs={{0,8},{2,10},{4,12},{6,14},{8,0},{10,2},{12,4},{14,6},{1,9},{3,11}... | collective-permute-start | bytes 196616 | tf_op jit(solution)/shard_map/ppermute | solution.py:174
  65.1 8.9 %collective-permute-start.9 = (f16[8,32,128]{2,0,1:T(8,128)(2,1)S(1)}, f16[8,32,128]{2,0,1:T(8,128)(2,1)S(1)}, u32[]{:S(2)}, u32[]{:S(2)}) collective-permute-start(f16[8,32,128]{2,0,1:T(8,128)(2,1)S(1)} %fusion.34), channel_id=1, source_target_pairs={{0,8},{2,10},{4,12},{6,14},{8,0},{10,2},{12,4},{14,6},{1,9},{3,11}... | collective-permute-start | bytes 196616 | tf_op jit(solution)/shard_map/ppermute | solution.py:174
  66.0 8.8 %collective-permute-start.3 = (f16[8,32,128]{2,0,1:T(8,128)(2,1)S(1)}, f16[8,32,128]{2,0,1:T(8,128)(2,1)S(1)}, u32[]{:S(2)}, u32[]{:S(2)}) collective-permute-start(f16[8,32,128]{2,0,1:T(8,128)(2,1)S(1)} %fusion.32), channel_id=1, source_target_pairs={{0,8},{2,10},{4,12},{6,14},{8,0},{10,2},{12,4},{14,6},{1,9},{3,11}... | collective-permute-start | bytes 196616 | tf_op jit(solution)/shard_map/ppermute | solution.py:174
  69.1 6.4 %collective-permute-start.6 = (f16[8,32,128]{2,0,1:T(8,128)(2,1)S(1)}, f16[8,32,128]{2,0,1:T(8,128)(2,1)S(1)}, u32[]{:S(2)}, u32[]{:S(2)}) collective-permute-start(f16[8,32,128]{2,0,1:T(8,128)(2,1)S(1)} %fusion.33), channel_id=1, source_target_pairs={{0,8},{2,10},{4,12},{6,14},{8,0},{10,2},{12,4},{14,6},{1,9},{3,11}... | collective-permute-start | bytes 196616 | tf_op jit(solution)/shard_map/ppermute | solution.py:174
where the time goes:
time: 76.6 us; the launch traced here: 76.3 us
  Pallas kernels  35 us (46%)
  starting transfers between devices  18.2 us (24%)
  waiting for transfers between devices  11 us (14%)
  local copies, waits for them, and re-layouts  5.88 us (8%)
  other arithmetic  4.68 us (6%)
  between operations  1.59 us (2%)
    pallas_call x1, Pallas kernels, paganin_thickness(): pl.pallas_call(filter_kernel, grid=(angles,), out_shape=jax.ShapeDtypeStr...  21 us
    ppermute x12, starting transfers between devices, butterfly(): came = lax.ppermute((send * scale).astype(link_type), 'angle', pairs)  17.7 us
    pallas_call x4, Pallas kernels, backproject(): pl.pallas_call(functools.partial(backproject_kernel, first), out_shape=ja...  14 us
    ppermute x12, waiting for transfers between devices, butterfly(): came = lax.ppermute((send * scale).astype(link_type), 'angle', pairs)  10.2 us
    unnamed x14, local copies, waits for them, and re-layouts  4.74 us
  transfers between devices with their start and end apart: 13, of which 7 were waited for; matrix products, arithmetic and copies ran while one was open for 6% of the time, Pallas kernels for 14%

commit v1 on v0

--- a/solution.py
+++ b/solution.py
@@ -12,6 +12,8 @@
 paganin_alpha = 2.0
 link_type = jnp.float16
 chunk_total = 4
+pitch_extra = 9
+unroll_blocks = 4
 
 
 def split_pair(array):
@@ -20,63 +22,64 @@
     return high, low
 
 
-def filter_tables(row_total):
+def filter_tables(row_total, edge):
     index = np.arange(row_total)
     phase = 2.0 * np.pi * (index[:, None] * index[None, :] % row_total) / row_total
     hartley = (np.cos(phase) + np.sin(phase)) / math.sqrt(row_total)
-    high = hartley.astype(np.float32).astype(jnp.bfloat16)
-    low = (hartley - high.astype(np.float64)).astype(np.float32).astype(jnp.bfloat16)
     a = 1.0 + paganin_alpha * (4.0 * np.sin(np.pi * index / row_total) ** 2 + 2.0)
     pole = (a - np.sqrt(a * a - 4.0 * paganin_alpha**2)) / (2.0 * paganin_alpha)
     gain = pole / (paganin_alpha * (1.0 - pole * pole))
+
+    def halves(matrix):
+        high = matrix.astype(np.float32).astype(jnp.bfloat16)
+        return high, (matrix - high.astype(np.float64)).astype(np.float32).astype(jnp.bfloat16)
+
+    high, low = halves(hartley * gain[None, :])
     forward = np.concatenate([np.concatenate([high, low], 1)] * 2, 0)
+    high, low = halves(hartley)
     inverse = np.concatenate([np.concatenate([high, high], 1), np.concatenate([low, low], 1)], 0)
-    poles = np.stack([pole, gain]).astype(np.float32)
-    return forward, inverse, poles
-
-
-def filter_kernel(x_ref, forward_ref, inverse_ref, pole_ref, out_ref, spectrum, causal):
+    reach = pole[None, :] ** np.arange(1, edge + 1)[:, None]
+    powers = np.concatenate([reach, reach[::-1]], 0).astype(np.float32)
+    return forward, inverse, powers
+
+
+def filter_kernel(x_ref, forward_ref, inverse_ref, power_ref, out_ref, spectrum, ahead_ref, behind_ref, ends):
     edge = out_ref.shape[-1]
     segments = out_ref.shape[1]
     rows = out_ref.shape[2]
+    pitch = edge + pitch_extra
     for s in range(segments):
         high, low = split_pair(x_ref[0, :, s * edge : (s + 1) * edge])
         both = jnp.concatenate([high, low], axis=0)
         product = lax.dot_general(
             both, forward_ref[...], (((0,), (0,)), ((), ())), preferred_element_type=jnp.float32
         )
-        spectrum[s * edge : (s + 1) * edge, :] = product[:, :rows] + product[:, rows:]
-    pole = jnp.broadcast_to(pole_ref[0:1, :], (segments, rows))
-    gain = jnp.broadcast_to(pole_ref[1:2, :], (segments, rows))
+        spectrum[s * pitch : s * pitch + edge, :] = product[:, :rows] + product[:, rows:]
+    pole = jnp.broadcast_to(power_ref[0:1, :], (segments, rows))
     zero = jnp.zeros((segments, rows), jnp.float32)
 
     def column(t):
-        return pl.ds(t, segments, stride=edge)
-
-    def warm(t, state):
-        ahead, behind = state
-        return (
-            ahead * pole + spectrum[column(t), :],
-            behind * pole + spectrum[column(edge - 1 - t), :],
-        )
-
-    ahead, behind = lax.fori_loop(0, edge, warm, (zero, zero), unroll=8)
-    ahead = jnp.concatenate([ahead[segments - 1 :], ahead[: segments - 1]], axis=0)
-    behind = jnp.concatenate([behind[1:], behind[:1]], axis=0)
+        return pl.ds(t, segments, stride=pitch)
 
     def sweep(t, state):
         ahead, behind = state
         ahead = ahead * pole + spectrum[column(t), :]
-        causal[0, column(t), :] = ahead * gain
+        ahead_ref[column(t), :] = ahead
         back = edge - 1 - t
         behind = behind * pole
-        causal[1, column(back), :] = behind * gain
+        behind_ref[column(back), :] = behind
         return ahead, behind + spectrum[column(back), :]
 
-    lax.fori_loop(0, edge, sweep, (ahead, behind), unroll=8)
+    ahead, behind = lax.fori_loop(0, edge, sweep, (zero, zero), unroll=16)
+    ends[0] = ahead
+    ends[1] = behind
     for s in range(segments):
-        span = slice(s * edge, (s + 1) * edge)
-        high, low = split_pair(causal[0, span, :] + causal[1, span, :])
+        span = slice(s * pitch, s * pitch + edge)
+        before, after = (s - 1) % segments, (s + 1) % segments
+        value = ahead_ref[span, :] + behind_ref[span, :]
+        value = value + power_ref[:edge, :] * ends[0, before : before + 1, :]
+        value = value + power_ref[edge:, :] * ends[1, after : after + 1, :]
+        high, low = split_pair(value)
         both = jnp.concatenate([high, low], axis=1)
         product = lax.dot_general(
             inverse_ref[...], both, (((1,), (1,)), ((), ())), preferred_element_type=jnp.float32
@@ -86,9 +89,10 @@
 
 def paganin_thickness(intensity, edge):
     angles, rows, width = intensity.shape
-    forward, inverse, poles = filter_tables(rows)
+    forward, inverse, powers = filter_tables(rows, edge)
     segments = width // edge
     whole = lambda *shape: pl.BlockSpec(shape, lambda a: (0,) * len(shape))
+    plane = pltpu.VMEM((segments * (edge + pitch_extra), rows), jnp.float32)
     return pl.pallas_call(
         filter_kernel,
         grid=(angles,),
@@ -97,44 +101,45 @@
             pl.BlockSpec((1, rows, width), lambda a: (a, 0, 0)),
             whole(2 * rows, 2 * rows),
             whole(2 * rows, 2 * rows),
-            whole(2, rows),
+            whole(2 * edge, rows),
         ],
         out_specs=pl.BlockSpec((1, segments, rows, edge), lambda a: (a, 0, 0, 0)),
-        scratch_shapes=[
-            pltpu.VMEM((width, rows), jnp.float32),
-            pltpu.VMEM((2, width, rows), jnp.float32),
-        ],
-        compiler_params=pltpu.CompilerParams(vmem_limit_bytes=32 * 2**20),
+        scratch_shapes=[plane, plane, plane, pltpu.VMEM((2, segments, rows), jnp.float32)],
+        compiler_params=pltpu.CompilerParams(vmem_limit_bytes=60 * 2**20),
         name="paganin_filter",
-    )(intensity, jnp.asarray(forward), jnp.asarray(inverse), jnp.asarray(poles))
+    )(intensity, jnp.asarray(forward), jnp.asarray(inverse), jnp.asarray(powers))
 
 
 def backproject_kernel(first, seg_ref, tile_ref, order_ref, start_ref, count_ref, *refs):
     *thick_refs, tiles_ref, out_ref, rows_ref = refs
     groups, block_total, capacity, edge = out_ref.shape
     angles, _, rows, _ = thick_refs[0].shape
-    rows_ref[rows:, :] = jnp.zeros((rows_ref.shape[0] - rows, edge), jnp.float32)
+    lanes = math.gcd(unroll_blocks, block_total)
+    for lane in range(lanes):
+        rows_ref[lane, rows:, :] = jnp.zeros((capacity, edge), jnp.float32)
     slot = lax.broadcasted_iota(jnp.int32, (capacity, edge), 0)
 
-    def one_block(v, _):
-        block = order_ref[first + v]
-        pieces, maps = [], []
-        for source, thick in enumerate(thick_refs):
-            for a in range(angles):
-                row = source * angles + a
-                pieces.append(thick[a, seg_ref[row, block]])
-                maps.append(tiles_ref[tile_ref[row, block]])
-        rows_ref[:rows, :] = jnp.dot(
-            jnp.concatenate(pieces, axis=1),
-            jnp.concatenate(maps, axis=0),
-            preferred_element_type=jnp.float32,
-        )
-        for g in range(groups):
-            picked = rows_ref[pl.ds(start_ref[g], capacity), :]
-            out_ref[g, v] = jnp.where(slot < count_ref[g], picked, 0.0)
+    def some_blocks(step, _):
+        for lane in range(lanes):
+            v = step * lanes + lane
+            block = order_ref[first + v]
+            pieces, maps = [], []
+            for source, thick in enumerate(thick_refs):
+                for a in range(angles):
+                    row = source * angles + a
+                    pieces.append(thick[a, seg_ref[row, block]])
+                    maps.append(tiles_ref[tile_ref[row, block]])
+            rows_ref[lane, :rows, :] = jnp.dot(
+                jnp.concatenate(pieces, axis=1),
+                jnp.concatenate(maps, axis=0),
+                preferred_element_type=jnp.float32,
+            )
+            for g in range(groups):
+                picked = rows_ref[lane, pl.ds(start_ref[g], capacity), :]
+                out_ref[g, v] = jnp.where(slot < count_ref[g], picked, 0.0)
         return 0
 
-    lax.fori_loop(0, block_total, one_block, 0)
+    lax.fori_loop(0, block_total // lanes, some_blocks, 0)
 
 
 def backproject(thick, seg_rows, tile_rows, order, starts, counts, tiles, first, blocks, capacity):
@@ -148,7 +153,7 @@
         out_shape=jax.ShapeDtypeStruct((groups, blocks, capacity, edge), jnp.float32),
         in_specs=[smem] * 5 + [vmem] * (len(thick) + 1),
         out_specs=vmem,
-        scratch_shapes=[pltpu.VMEM((rows + capacity, edge), jnp.float32)],
+        scratch_shapes=[pltpu.VMEM((unroll_blocks, rows + capacity, edge), jnp.float32)],
         compiler_params=pltpu.CompilerParams(vmem_limit_bytes=32 * 2**20),
         cost_estimate=pl.CostEstimate(
             flops=flops, bytes_accessed=4 * groups * blocks * capacity * edge, transcendentals=0

time: 76.6 us -> 54.6 us (0.71)
  Pallas kernels: 35 us -> 15.2 us
  local copies, waits for them, and re-layouts: 5.88 us -> 2.73 us
  waiting for transfers between devices: 11 us -> 12.3 us
    pallas_call x1, Pallas kernels: 21 us -> 8.62 us  [paganin_thickness(): pl.pallas_call(filter_kernel, grid=(angles,), out_shape=jax.ShapeDtypeStr...]
    pallas_call x4, Pallas kernels: 14 us -> 6.62 us  [backproject(): pl.pallas_call(functools.partial(backproject_kernel, first), out_shape=ja...]
    unnamed x14 -> x8, local copies, waits for them, and re-layouts: 4.74 us -> 1.6 us
    ppermute x12, waiting for transfers between devices: 10.2 us -> 11.4 us  [butterfly(): came = lax.ppermute((send * scale).astype(link_type), 'angle', pairs)]
  transfers between devices with their start and end apart: 13 -> 13, of which waited for: 7 -> 6; matrix products, arithmetic and copies ran while one was open for 6% -> 8% of each run, Pallas kernels for 14% -> 9%
where the time goes in v1:
time: 54.6 us; the launch traced here: 54.3 us
  starting transfers between devices  17.8 us (33%)
  Pallas kernels  15.2 us (28%)
  waiting for transfers between devices  12.3 us (23%)
  other arithmetic  4.69 us (9%)
  local copies, waits for them, and re-layouts  2.73 us (5%)
  between operations  1.57 us (3%)
    ppermute x12, starting transfers between devices, butterfly(): came = lax.ppermute((send * scale).astype(link_type), 'angle', pairs)  17.3 us
    ppermute x12, waiting for transfers between devices, butterfly(): came = lax.ppermute((send * scale).astype(link_type), 'angle', pairs)  11.4 us
    pallas_call x1, Pallas kernels, paganin_thickness(): pl.pallas_call(filter_kernel, grid=(angles,), out_shape=jax.ShapeDtypeStr...  8.62 us
    pallas_call x4, Pallas kernels, backproject(): pl.pallas_call(functools.partial(backproject_kernel, first), out_shape=ja...  6.62 us
    unnamed x8, local copies, waits for them, and re-layouts  1.6 us
    add x12, other arithmetic, butterfly(): current = keep + came.astype(jnp.float32) / scale  1.54 us
    convert_element_type x12, other arithmetic, butterfly(): came = lax.ppermute((send * scale).astype(link_type), 'angle', pairs)  1.45 us
  transfers between devices with their start and end apart: 13, of which 6 were waited for; matrix products, arithmetic and copies ran while one was open for 8% of the time, Pallas kernels for 9%

profile of v1, /device:TPU:0, one launch (start us, length us, event | category | flops | bytes accessed | tf_op | source)
XLA Modules:
  0.0 54.3 jit_solution(2026265269537378338)
XLA Ops:
  0.0 8.6 %paganin_filter.1.refs_0_ = bf16[4,16,128,128]{3,2,1,0:T(8,128)(2,1)} custom-call(f32[4,128,2048]{2,1,0:T(8,128)} %x_ref.1, bf16[256,256]{1,0:T(8,128)(2,1)} %constant.47.clone.forward_ref, bf16[256,256]{1,0:T(8,128)(2,1)} %constant.48.clone.inverse_ref, f32[256,128]{1,0:T(8,128)} %constant.49.clone.power_ref), custom_call_target="tpu_custom_call" | custom-call | tf_op jit(solution)/shard_map/paganin_filter/pallas_call | solution.py:96
  8.6 0.5 collective-permute-start
  9.1 0.7 %abs_reduce_fusion = f32[]{:T(128)} fusion(bf16[16,128,128]{2,1,0:T(8,128)(2,1)S(1)} %copy-done.1), kind=kLoop, calls=%fused_computation | loop fusion | flops 786431 | bytes 524292 | tf_op jit(solution)/shard_map/reduce_max | solution.py:215
  11.2 0.8 %constant_dynamic-slice_fusion.1 = (s32[4,64]{1,0:T(4,128)S(1)}, s32[4,64]{1,0:T(4,128)S(1)}, s32[4,64]{1,0:T(4,128)S(1)}, s32[4,64]{1,0:T(4,128)S(1)}) fusion(s32[64,64]{1,0:T(8,128)} %param.12, s32[]{:T(128)S(6)} %select_n.29, s32[]{:T(128)S(6)} %select_n.31, s32[64,64]{1,0:T(8,128)} %param.11), kind=kLoop, calls=%fused_computation.69 | loop fusion | bytes 8200 | tf_op jit(solution)/shard_map/dynamic_slice | solution.py:206
  12.2 0.9 %collective-permute-done.refs_1_ = bf16[4,16,128,128]{3,2,1,0:T(8,128)(2,1)S(1)} collective-permute-done((bf16[4,16,128,128]{3,2,1,0:T(8,128)(2,1)}, bf16[4,16,128,128]{3,2,1,0:T(8,128)(2,1)S(1)}, u32[]{:S(2)}, u32[]{:S(2)}) %collective-permute-start) | collective-permute-done | bytes 2097184 | tf_op jit(solution)/shard_map/ppermute | solution.py:199
  13.1 1.6 %copy-done = bf16[4,16,128,128]{3,2,1,0:T(8,128)(2,1)S(1)} copy-done((bf16[4,16,128,128]{3,2,1,0:T(8,128)(2,1)S(1)}, bf16[4,16,128,128]{3,2,1,0:T(8,128)(2,1)}, u32[]{:S(2)}) %copy-start) | copy-done | bytes 2097176
  14.7 1.7 %backproject.7 = f32[8,8,32,128]{3,2,1,0:T(8,128)S(1)} custom-call(s32[8,64]{1,0:T(8,128)S(1)} %pad_add_fusion.seg_ref, s32[8,64]{1,0:T(8,128)S(1)} %pad_add_fusion.1.tile_ref, s32[32]{0:T(128)S(1)} %dynamic_slice.19.order_ref, s32[8]{0:T(128)S(1)} %get-tuple-element.6.start_ref, s32[8]{0:T(128)S(1)} %get-tuple-element.5.count_ref, ...), custom_call_target="tpu_custom_call" | custom-call | flops 268435456 | bytes 1048576 | tf_op jit(solution)/shard_map/backproject/pallas_call | solution.py:151
  16.7 3.0 %collective-permute-start.10 = (f16[2,2,8,32,128]{4,2,3,0,1:T(8,128)(2,1)S(1)}, f16[2,2,8,32,128]{4,2,3,0,1:T(8,128)(2,1)S(1)}, u32[]{:S(2)}, u32[]{:S(2)}) collective-permute-start(f16[2,2,8,32,128]{4,2,3,0,1:T(8,128)(2,1)S(1)} %fusion.11), channel_id=1, source_target_pairs={{0,4},{2,6},{4,0},{6,2},{8,12},{10,14},{12,8},{14,10},{1,5},{3,7},... | collective-permute-start | bytes 786440 | tf_op jit(solution)/shard_map/ppermute | solution.py:179
  19.8 1.7 %backproject.6 = f32[8,8,32,128]{3,2,1,0:T(8,128)S(1)} custom-call(s32[8,64]{1,0:T(8,128)S(1)} %pad_add_fusion.seg_ref, s32[8,64]{1,0:T(8,128)S(1)} %pad_add_fusion.1.tile_ref, s32[32]{0:T(128)S(1)} %dynamic_slice.19.order_ref, s32[8]{0:T(128)S(1)} %get-tuple-element.6.start_ref, s32[8]{0:T(128)S(1)} %get-tuple-element.5.count_ref, ...), custom_call_target="tpu_custom_call" | custom-call | flops 268435456 | bytes 1048576 | tf_op jit(solution)/shard_map/backproject/pallas_call | solution.py:151
  21.5 0.3 fusion.10
  21.8 1.6 %collective-permute-start.7 = (f16[2,2,8,32,128]{4,2,3,0,1:T(8,128)(2,1)S(1)}, f16[2,2,8,32,128]{4,2,3,0,1:T(8,128)(2,1)S(1)}, u32[]{:S(2)}, u32[]{:S(2)}) collective-permute-start(f16[2,2,8,32,128]{4,2,3,0,1:T(8,128)(2,1)S(1)} %fusion.10), channel_id=1, source_target_pairs={{0,2},{2,0},{4,6},{6,4},{8,10},{10,8},{12,14},{14,12},{1,3},{3,1},... | collective-permute-start | bytes 786440 | tf_op jit(solution)/shard_map/ppermute | solution.py:179
  23.4 1.7 %backproject.5 = f32[8,8,32,128]{3,2,1,0:T(8,128)S(1)} custom-call(s32[8,64]{1,0:T(8,128)S(1)} %pad_add_fusion.seg_ref, s32[8,64]{1,0:T(8,128)S(1)} %pad_add_fusion.1.tile_ref, s32[32]{0:T(128)S(1)} %dynamic_slice.19.order_ref, s32[8]{0:T(128)S(1)} %get-tuple-element.6.start_ref, s32[8]{0:T(128)S(1)} %get-tuple-element.5.count_ref, ...), custom_call_target="tpu_custom_call" | custom-call | flops 268435456 | bytes 1048576 | tf_op jit(solution)/shard_map/backproject/pallas_call | solution.py:151
  25.1 1.7 %backproject.4 = f32[8,8,32,128]{3,2,1,0:T(8,128)S(1)} custom-call(s32[8,64]{1,0:T(8,128)S(1)} %pad_add_fusion.seg_ref, s32[8,64]{1,0:T(8,128)S(1)} %pad_add_fusion.1.tile_ref, s32[32]{0:T(128)S(1)} %dynamic_slice.19.order_ref, s32[8]{0:T(128)S(1)} %get-tuple-element.6.start_ref, s32[8]{0:T(128)S(1)} %get-tuple-element.5.count_ref, ...), custom_call_target="tpu_custom_call" | custom-call | flops 268435456 | bytes 1048576 | tf_op jit(solution)/shard_map/backproject/pallas_call | solution.py:151
  27.2 0.6 %collective-permute-start.1 = (f16[2,2,8,32,128]{4,2,3,0,1:T(8,128)(2,1)S(1)}, f16[2,2,8,32,128]{4,2,3,0,1:T(8,128)(2,1)S(1)}, u32[]{:S(2)}, u32[]{:S(2)}) collective-permute-start(f16[2,2,8,32,128]{4,2,3,0,1:T(8,128)(2,1)S(1)} %fusion.8), channel_id=1, source_target_pairs={{0,2},{2,0},{4,6},{6,4},{8,10},{10,8},{12,14},{14,12},{1,3},{3,1},... | collective-permute-start | bytes 786440 | tf_op jit(solution)/shard_map/ppermute | solution.py:179
  28.2 0.3 fusion.1
  28.6 2.0 %collective-permute-start.11 = (f16[2,8,32,128]{3,1,2,0:T(8,128)(2,1)S(1)}, f16[2,8,32,128]{3,1,2,0:T(8,128)(2,1)S(1)}, u32[]{:S(2)}, u32[]{:S(2)}) collective-permute-start(f16[2,8,32,128]{3,1,2,0:T(8,128)(2,1)S(1)} %fusion.23), channel_id=1, source_target_pairs={{0,2},{2,0},{4,6},{6,4},{8,10},{10,8},{12,14},{14,12},{1,3},{3,1},... | collective-permute-start | bytes 393224 | tf_op jit(solution)/shard_map/ppermute | solution.py:179
  30.6 0.3 fusion.3
  30.9 1.6 %collective-permute-start.8 = (f16[2,8,32,128]{3,1,2,0:T(8,128)(2,1)S(1)}, f16[2,8,32,128]{3,1,2,0:T(8,128)(2,1)S(1)}, u32[]{:S(2)}, u32[]{:S(2)}) collective-permute-start(f16[2,8,32,128]{3,1,2,0:T(8,128)(2,1)S(1)} %fusion.22), channel_id=1, source_target_pairs={{0,4},{2,6},{4,0},{6,2},{8,12},{10,14},{12,8},{14,10},{1,5},{3,7},... | collective-permute-start | bytes 393224 | tf_op jit(solution)/shard_map/ppermute | solution.py:179
  32.6 3.9 %collective-permute-done.1 = f16[2,2,8,32,128]{4,2,3,0,1:T(8,128)(2,1)S(1)} collective-permute-done((f16[2,2,8,32,128]{4,2,3,0,1:T(8,128)(2,1)S(1)}, f16[2,2,8,32,128]{4,2,3,0,1:T(8,128)(2,1)S(1)}, u32[]{:S(2)}, u32[]{:S(2)}) %collective-permute-start.1) | collective-permute-done | bytes 262176 | tf_op jit(solution)/shard_map/ppermute | solution.py:179
  36.5 0.3 fusion.7
  36.9 0.5 collective-permute-start.2
  37.4 0.3 fusion.5
  37.8 1.8 %collective-permute-start.5 = (f16[2,8,32,128]{3,1,2,0:T(8,128)(2,1)S(1)}, f16[2,8,32,128]{3,1,2,0:T(8,128)(2,1)S(1)}, u32[]{:S(2)}, u32[]{:S(2)}) collective-permute-start(f16[2,8,32,128]{3,1,2,0:T(8,128)(2,1)S(1)} %fusion.21), channel_id=1, source_target_pairs={{0,2},{2,0},{4,6},{6,4},{8,10},{10,8},{12,14},{14,12},{1,3},{3,1},... | collective-permute-start | bytes 393224 | tf_op jit(solution)/shard_map/ppermute | solution.py:179
  39.6 2.7 %collective-permute-start.12 = (f16[8,32,128]{2,0,1:T(8,128)(2,1)S(1)}, f16[8,32,128]{2,0,1:T(8,128)(2,1)S(1)}, u32[]{:S(2)}, u32[]{:S(2)}) collective-permute-start(f16[8,32,128]{2,0,1:T(8,128)(2,1)S(1)} %fusion.35), channel_id=1, source_target_pairs={{0,8},{2,10},{4,12},{6,14},{8,0},{10,2},{12,4},{14,6},{1,9},{3,11}... | collective-permute-start | bytes 196616 | tf_op jit(solution)/shard_map/ppermute | solution.py:179
  42.3 0.4 collective-permute-start.9
  42.8 2.7 %collective-permute-start.3 = (f16[8,32,128]{2,0,1:T(8,128)(2,1)S(1)}, f16[8,32,128]{2,0,1:T(8,128)(2,1)S(1)}, u32[]{:S(2)}, u32[]{:S(2)}) collective-permute-start(f16[8,32,128]{2,0,1:T(8,128)(2,1)S(1)} %fusion.32), channel_id=1, source_target_pairs={{0,8},{2,10},{4,12},{6,14},{8,0},{10,2},{12,4},{14,6},{1,9},{3,11}... | collective-permute-start | bytes 196616 | tf_op jit(solution)/shard_map/ppermute | solution.py:179
  45.5 0.4 collective-permute-start.6
  45.9 3.7 %collective-permute-done.12 = f16[8,32,128]{2,0,1:T(8,128)(2,1)S(1)} collective-permute-done((f16[8,32,128]{2,0,1:T(8,128)(2,1)S(1)}, f16[8,32,128]{2,0,1:T(8,128)(2,1)S(1)}, u32[]{:S(2)}, u32[]{:S(2)}) %collective-permute-start.12) | collective-permute-done | bytes 65568 | tf_op jit(solution)/shard_map/ppermute | solution.py:179
  49.6 1.4 %collective-permute-done.9 = f16[8,32,128]{2,0,1:T(8,128)(2,1)S(1)} collective-permute-done((f16[8,32,128]{2,0,1:T(8,128)(2,1)S(1)}, f16[8,32,128]{2,0,1:T(8,128)(2,1)S(1)}, u32[]{:S(2)}, u32[]{:S(2)}) %collective-permute-start.9) | collective-permute-done | bytes 65568 | tf_op jit(solution)/shard_map/ppermute | solution.py:179
  51.0 1.7 %collective-permute-done.3 = f16[8,32,128]{2,0,1:T(8,128)(2,1)S(1)} collective-permute-done((f16[8,32,128]{2,0,1:T(8,128)(2,1)S(1)}, f16[8,32,128]{2,0,1:T(8,128)(2,1)S(1)}, u32[]{:S(2)}, u32[]{:S(2)}) %collective-permute-start.3) | collective-permute-done | bytes 65568 | tf_op jit(solution)/shard_map/ppermute | solution.py:179
  52.8 0.7 %collective-permute-done.6 = f16[8,32,128]{2,0,1:T(8,128)(2,1)S(1)} collective-permute-done((f16[8,32,128]{2,0,1:T(8,128)(2,1)S(1)}, f16[8,32,128]{2,0,1:T(8,128)(2,1)S(1)}, u32[]{:S(2)}, u32[]{:S(2)}) %collective-permute-start.6) | collective-permute-done | bytes 65568 | tf_op jit(solution)/shard_map/ppermute | solution.py:179
  53.5 0.8 %maximum_bitcast_fusion = f32[1,32,32,128]{3,2,1,0:T(8,128)} fusion(f32[8,32,128]{2,0,1:T(8,128)S(1)} %fusion.25, f32[8,32,128]{2,0,1:T(8,128)S(1)} %fusion.27, f32[8,32,128]{2,0,1:T(8,128)S(1)} %fusion.29, f32[8,32,128]{2,0,1:T(8,128)S(1)} %fusion.31), kind=kLoop, calls=%fused_computation.1 | loop fusion | flops 393216 | bytes 1048576 | tf_op jit(solution)/shard_map/broadcast_in_dim | solution.py:229
  (43 shorter events, 2.1 us)
Async XLA Ops:
  0.0 9.1 %copy-start.1 = (bf16[16,128,128]{2,1,0:T(8,128)(2,1)S(1)}, bf16[16,128,128]{2,1,0:T(8,128)(2,1)}, u32[]{:S(2)}) copy-start(bf16[16,128,128]{2,1,0:T(8,128)(2,1)} %refs_2_.7) | copy-start | bytes 1572868
  0.0 11.1 %copy-start.3 = (s32[64]{0:T(128)S(1)}, s32[64]{0:T(128)}, u32[]{:S(2)}) copy-start(s32[64]{0:T(128)} %param.13) | copy-start | bytes 772
  0.0 12.0 %copy-start.2 = (s32[8]{0:T(128)S(1)}, s32[8]{0:T(128)}, u32[]{:S(2)}) copy-start(s32[8]{0:T(128)} %param.10) | copy-start | bytes 100
  8.6 4.5 %collective-permute-start = (bf16[4,16,128,128]{3,2,1,0:T(8,128)(2,1)}, bf16[4,16,128,128]{3,2,1,0:T(8,128)(2,1)S(1)}, u32[]{:S(2)}, u32[]{:S(2)}) collective-permute-start(bf16[4,16,128,128]{3,2,1,0:T(8,128)(2,1)} %paganin_filter.1.refs_0_), channel_id=1, source_target_pairs={{0,1},{1,0},{2,3},{3,2},{4,5},{5,4},{6,7},{7,6},{8,9},{9,8},{10,11... | collective-permute-start | bytes 6291464 | tf_op jit(solution)/shard_map/ppermute | solution.py:199
  13.1 1.6 %copy-start = (bf16[4,16,128,128]{3,2,1,0:T(8,128)(2,1)S(1)}, bf16[4,16,128,128]{3,2,1,0:T(8,128)(2,1)}, u32[]{:S(2)}) copy-start(bf16[4,16,128,128]{3,2,1,0:T(8,128)(2,1)} %paganin_filter.1.refs_0_) | copy-start | bytes 6291460
  16.7 11.4 %collective-permute-start.10 = (f16[2,2,8,32,128]{4,2,3,0,1:T(8,128)(2,1)S(1)}, f16[2,2,8,32,128]{4,2,3,0,1:T(8,128)(2,1)S(1)}, u32[]{:S(2)}, u32[]{:S(2)}) collective-permute-start(f16[2,2,8,32,128]{4,2,3,0,1:T(8,128)(2,1)S(1)} %fusion.11), channel_id=1, source_target_pairs={{0,4},{2,6},{4,0},{6,2},{8,12},{10,14},{12,8},{14,10},{1,5},{3,7},... | collective-permute-start | bytes 786440 | tf_op jit(solution)/shard_map/ppermute | solution.py:179
  21.8 8.8 %collective-permute-start.7 = (f16[2,2,8,32,128]{4,2,3,0,1:T(8,128)(2,1)S(1)}, f16[2,2,8,32,128]{4,2,3,0,1:T(8,128)(2,1)S(1)}, u32[]{:S(2)}, u32[]{:S(2)}) collective-permute-start(f16[2,2,8,32,128]{4,2,3,0,1:T(8,128)(2,1)S(1)} %fusion.10), channel_id=1, source_target_pairs={{0,2},{2,0},{4,6},{6,4},{8,10},{10,8},{12,14},{14,12},{1,3},{3,1},... | collective-permute-start | bytes 786440 | tf_op jit(solution)/shard_map/ppermute | solution.py:179
  27.2 9.3 %collective-permute-start.1 = (f16[2,2,8,32,128]{4,2,3,0,1:T(8,128)(2,1)S(1)}, f16[2,2,8,32,128]{4,2,3,0,1:T(8,128)(2,1)S(1)}, u32[]{:S(2)}, u32[]{:S(2)}) collective-permute-start(f16[2,2,8,32,128]{4,2,3,0,1:T(8,128)(2,1)S(1)} %fusion.8), channel_id=1, source_target_pairs={{0,2},{2,0},{4,6},{6,4},{8,10},{10,8},{12,14},{14,12},{1,3},{3,1},... | collective-permute-start | bytes 786440 | tf_op jit(solution)/shard_map/ppermute | solution.py:179
  28.1 9.3 %collective-permute-start.4 = (f16[2,2,8,32,128]{4,2,3,0,1:T(8,128)(2,1)S(1)}, f16[2,2,8,32,128]{4,2,3,0,1:T(8,128)(2,1)S(1)}, u32[]{:S(2)}, u32[]{:S(2)}) collective-permute-start(f16[2,2,8,32,128]{4,2,3,0,1:T(8,128)(2,1)S(1)} %fusion.9), channel_id=1, source_target_pairs={{0,4},{2,6},{4,0},{6,2},{8,12},{10,14},{12,8},{14,10},{1,5},{3,7},... | collective-permute-start | bytes 786440 | tf_op jit(solution)/shard_map/ppermute | solution.py:179
  28.6 11.0 %collective-permute-start.11 = (f16[2,8,32,128]{3,1,2,0:T(8,128)(2,1)S(1)}, f16[2,8,32,128]{3,1,2,0:T(8,128)(2,1)S(1)}, u32[]{:S(2)}, u32[]{:S(2)}) collective-permute-start(f16[2,8,32,128]{3,1,2,0:T(8,128)(2,1)S(1)} %fusion.23), channel_id=1, source_target_pairs={{0,2},{2,0},{4,6},{6,4},{8,10},{10,8},{12,14},{14,12},{1,3},{3,1},... | collective-permute-start | bytes 393224 | tf_op jit(solution)/shard_map/ppermute | solution.py:179
  30.9 11.3 %collective-permute-start.8 = (f16[2,8,32,128]{3,1,2,0:T(8,128)(2,1)S(1)}, f16[2,8,32,128]{3,1,2,0:T(8,128)(2,1)S(1)}, u32[]{:S(2)}, u32[]{:S(2)}) collective-permute-start(f16[2,8,32,128]{3,1,2,0:T(8,128)(2,1)S(1)} %fusion.22), channel_id=1, source_target_pairs={{0,4},{2,6},{4,0},{6,2},{8,12},{10,14},{12,8},{14,10},{1,5},{3,7},... | collective-permute-start | bytes 393224 | tf_op jit(solution)/shard_map/ppermute | solution.py:179
  36.9 5.9 %collective-permute-start.2 = (f16[2,8,32,128]{3,1,2,0:T(8,128)(2,1)S(1)}, f16[2,8,32,128]{3,1,2,0:T(8,128)(2,1)S(1)}, u32[]{:S(2)}, u32[]{:S(2)}) collective-permute-start(f16[2,8,32,128]{3,1,2,0:T(8,128)(2,1)S(1)} %fusion.20), channel_id=1, source_target_pairs={{0,4},{2,6},{4,0},{6,2},{8,12},{10,14},{12,8},{14,10},{1,5},{3,7},... | collective-permute-start | bytes 393224 | tf_op jit(solution)/shard_map/ppermute | solution.py:179
  37.8 7.7 %collective-permute-start.5 = (f16[2,8,32,128]{3,1,2,0:T(8,128)(2,1)S(1)}, f16[2,8,32,128]{3,1,2,0:T(8,128)(2,1)S(1)}, u32[]{:S(2)}, u32[]{:S(2)}) collective-permute-start(f16[2,8,32,128]{3,1,2,0:T(8,128)(2,1)S(1)} %fusion.21), channel_id=1, source_target_pairs={{0,2},{2,0},{4,6},{6,4},{8,10},{10,8},{12,14},{14,12},{1,3},{3,1},... | collective-permute-start | bytes 393224 | tf_op jit(solution)/shard_map/ppermute | solution.py:179
  39.6 10.0 %collective-permute-start.12 = (f16[8,32,128]{2,0,1:T(8,128)(2,1)S(1)}, f16[8,32,128]{2,0,1:T(8,128)(2,1)S(1)}, u32[]{:S(2)}, u32[]{:S(2)}) collective-permute-start(f16[8,32,128]{2,0,1:T(8,128)(2,1)S(1)} %fusion.35), channel_id=1, source_target_pairs={{0,8},{2,10},{4,12},{6,14},{8,0},{10,2},{12,4},{14,6},{1,9},{3,11}... | collective-permute-start | bytes 196616 | tf_op jit(solution)/shard_map/ppermute | solution.py:179
  42.3 8.7 %collective-permute-start.9 = (f16[8,32,128]{2,0,1:T(8,128)(2,1)S(1)}, f16[8,32,128]{2,0,1:T(8,128)(2,1)S(1)}, u32[]{:S(2)}, u32[]{:S(2)}) collective-permute-start(f16[8,32,128]{2,0,1:T(8,128)(2,1)S(1)} %fusion.34), channel_id=1, source_target_pairs={{0,8},{2,10},{4,12},{6,14},{8,0},{10,2},{12,4},{14,6},{1,9},{3,11}... | collective-permute-start | bytes 196616 | tf_op jit(solution)/shard_map/ppermute | solution.py:179
  42.8 10.0 %collective-permute-start.3 = (f16[8,32,128]{2,0,1:T(8,128)(2,1)S(1)}, f16[8,32,128]{2,0,1:T(8,128)(2,1)S(1)}, u32[]{:S(2)}, u32[]{:S(2)}) collective-permute-start(f16[8,32,128]{2,0,1:T(8,128)(2,1)S(1)} %fusion.32), channel_id=1, source_target_pairs={{0,8},{2,10},{4,12},{6,14},{8,0},{10,2},{12,4},{14,6},{1,9},{3,11}... | collective-permute-start | bytes 196616 | tf_op jit(solution)/shard_map/ppermute | solution.py:179
  45.5 7.9 %collective-permute-start.6 = (f16[8,32,128]{2,0,1:T(8,128)(2,1)S(1)}, f16[8,32,128]{2,0,1:T(8,128)(2,1)S(1)}, u32[]{:S(2)}, u32[]{:S(2)}) collective-permute-start(f16[8,32,128]{2,0,1:T(8,128)(2,1)S(1)} %fusion.33), channel_id=1, source_target_pairs={{0,8},{2,10},{4,12},{6,14},{8,0},{10,2},{12,4},{14,6},{1,9},{3,11}... | collective-permute-start | bytes 196616 | tf_op jit(solution)/shard_map/ppermute | solution.py:179

commit v2 on v1

--- a/solution.py
+++ b/solution.py
@@ -10,10 +10,13 @@
 from jax.sharding import PartitionSpec as P
 
 paganin_alpha = 2.0
-link_type = jnp.float16
-chunk_total = 4
+chunk_total = 8
+variant_every = 4
+lag = 2
+code_top = 32760.0
+round_shift = 12582912.0
+MESH = pl.DeviceIdType.MESH
 pitch_extra = 9
-unroll_blocks = 4
 
 
 def split_pair(array):
@@ -110,75 +113,203 @@
     )(intensity, jnp.asarray(forward), jnp.asarray(inverse), jnp.asarray(powers))
 
 
-def backproject_kernel(first, seg_ref, tile_ref, order_ref, start_ref, count_ref, *refs):
-    *thick_refs, tiles_ref, out_ref, rows_ref = refs
-    groups, block_total, capacity, edge = out_ref.shape
-    angles, _, rows, _ = thick_refs[0].shape
-    lanes = math.gcd(unroll_blocks, block_total)
-    for lane in range(lanes):
+def encode(value):
+    top = jnp.maximum(jnp.max(jnp.abs(value), axis=0, keepdims=True), 1e-30)
+    scaled = value * (code_top / top)
+    code = (scaled + round_shift) - round_shift
+    return code.astype(jnp.int32).astype(jnp.int16), top * (1.0 / code_top)
+
+
+def decode(code, unit):
+    return code.astype(jnp.int32).astype(jnp.float32) * unit
+
+
+def reduce_kernel(
+    stages, cores, chunks, seg_ref, tile_ref, order_ref, start_ref, count_ref, own, tiles_ref, out_ref,
+    other, rows_ref, part, kept, swap_send, swap_recv, data_send, data_recv, unit_send, unit_recv, *buffers
+):
+    send, came, send_unit, came_unit = (buffers[i * stages : (i + 1) * stages] for i in range(4))
+    groups = 2**stages
+    angles, _, rows, edge = own.shape
+    blocks, capacity, _ = out_ref.shape
+    per_chunk = blocks // chunks
+    place, core = lax.axis_index("angle"), lax.axis_index("tile")
+
+    def across(bit):
+        return place + (1 - 2 * ((place // (1 << bit)) % 2)) * (1 << bit)
+
+    partners = [across(bit) for bit in range(stages)]
+    neighbours = [lax.rem(core + step, cores) for step in range(1, cores)]
+    barrier = pltpu.get_barrier_semaphore()
+    for partner in partners:
+        pl.semaphore_signal(barrier, inc=1, device_id={"angle": partner}, device_id_type=MESH)
+    for neighbour in neighbours:
+        pl.semaphore_signal(barrier, inc=1, device_id={"tile": neighbour}, device_id_type=MESH)
+    pl.semaphore_wait(barrier, stages + cores - 1)
+
+    swaps = []
+    for index, neighbour in enumerate(neighbours):
+        for a in range(angles):
+            swaps.append(
+                pltpu.make_async_remote_copy(
+                    src_ref=own.at[a],
+                    dst_ref=other.at[index, a],
+                    send_sem=swap_send.at[index, a],
+                    recv_sem=swap_recv.at[index, a],
+                    device_id={"tile": neighbour},
+                    device_id_type=MESH,
+                )
+            )
+            swaps[-1].start()
+
+    for lane in range(per_chunk):
         rows_ref[lane, rows:, :] = jnp.zeros((capacity, edge), jnp.float32)
     slot = lax.broadcasted_iota(jnp.int32, (capacity, edge), 0)
 
-    def some_blocks(step, _):
-        for lane in range(lanes):
-            v = step * lanes + lane
-            block = order_ref[first + v]
-            pieces, maps = [], []
-            for source, thick in enumerate(thick_refs):
-                for a in range(angles):
-                    row = source * angles + a
-                    pieces.append(thick[a, seg_ref[row, block]])
-                    maps.append(tiles_ref[tile_ref[row, block]])
-            rows_ref[lane, :rows, :] = jnp.dot(
-                jnp.concatenate(pieces, axis=1),
-                jnp.concatenate(maps, axis=0),
-                preferred_element_type=jnp.float32,
+    def project(sources, first_row, block):
+        pieces, maps = [], []
+        for index, thick in enumerate(sources):
+            for a in range(angles):
+                row = first_row + index * angles + a
+                pieces.append(thick(a, seg_ref[row, block]))
+                maps.append(tiles_ref[tile_ref[row, block]])
+        return jnp.dot(
+            jnp.concatenate(pieces, axis=1),
+            jnp.concatenate(maps, axis=0),
+            preferred_element_type=jnp.float32,
+        )
+
+    def own_part(step, _):
+        for lane in range(per_chunk):
+            v = step * per_chunk + lane
+            part[v] = project([lambda a, s: own[a, s]], 0, order_ref[v])
+        return 0
+
+    lax.fori_loop(0, chunks, own_part, 0)
+    for swap in swaps:
+        swap.wait()
+    others = [lambda a, s, index=index: other[index, a, s] for index in range(cores - 1)]
+
+    def variant_of(c):
+        return (c % variant_every) // (variant_every - 1) if stages > 1 else 0
+
+    def copies(stage, c):
+        partner = partners[stage]
+        if stages > 1 and stage < 2:
+            variant = variant_of(c)
+            partner = partners[stage] * (1 - variant) + partners[1 - stage] * variant
+        made = []
+        for source, target, sent, got in (
+            (send[stage], came[stage], data_send, data_recv),
+            (send_unit[stage], came_unit[stage], unit_send, unit_recv),
+        ):
+            made.append(
+                pltpu.make_async_remote_copy(
+                    src_ref=source.at[c],
+                    dst_ref=target.at[c],
+                    send_sem=sent.at[stage, c],
+                    recv_sem=got.at[stage, c],
+                    device_id={"angle": partner},
+                    device_id_type=MESH,
+                )
             )
+        return made
+
+    def ship(stage, c, lane, position, value):
+        half = groups >> (stage + 1)
+        code, unit = encode(value)
+        send[stage][c, lane, position - half] = code
+        send_unit[stage][c, lane * half + position - half : lane * half + position - half + 1, :] = unit
+
+    def begin(c):
+        variant = variant_of(c)
+        for lane in range(per_chunk):
+            v = c * per_chunk + lane
+            rows_ref[lane, :rows, :] = part[v] + project(others, angles, order_ref[v])
+        for lane in range(per_chunk):
+            v = c * per_chunk + lane
             for g in range(groups):
-                picked = rows_ref[lane, pl.ds(start_ref[g], capacity), :]
-                out_ref[g, v] = jnp.where(slot < count_ref[g], picked, 0.0)
+                picked = rows_ref[lane, pl.ds(start_ref[variant, g], capacity), :]
+                picked = jnp.where(slot < count_ref[variant, g], picked, 0.0)
+                if g < groups // 2:
+                    kept[v, g] = picked
+                else:
+                    ship(0, c, lane, g, picked)
+        for copy in copies(0, c):
+            copy.start()
+
+    def advance(stage, c):
+        for copy in copies(stage - 1, c):
+            copy.wait()
+        left = groups >> stage
+        for lane in range(per_chunk):
+            v = c * per_chunk + lane
+            for g in range(left):
+                unit = came_unit[stage - 1][c, lane * left + g : lane * left + g + 1, :]
+                value = kept[v, g] + decode(came[stage - 1][c, lane, g], unit)
+                if stage == stages:
+                    out_ref[v] = value
+                elif g < left // 2:
+                    kept[v, g] = value
+                else:
+                    ship(stage, c, lane, g, value)
+        if stage < stages:
+            for copy in copies(stage, c):
+                copy.start()
+
+    def step_body(step, _):
+        @pl.when(step < chunks)
+        def _():
+            begin(step)
+
+        for stage in range(stages, 0, -1):
+            c = step - stage * lag
+
+            @pl.when((c >= 0) & (c < chunks))
+            def _(stage=stage, c=c):
+                advance(stage, c)
+
         return 0
 
-    lax.fori_loop(0, block_total // lanes, some_blocks, 0)
-
-
-def backproject(thick, seg_rows, tile_rows, order, starts, counts, tiles, first, blocks, capacity):
-    angles, segments, rows, edge = thick[0].shape
-    groups = starts.shape[0]
+    lax.fori_loop(0, chunks + stages * lag, step_body, 0)
+
+
+def reduced_blocks(thickness, seg_rows, tile_rows, order, starts, counts, tiles, capacity, cores):
+    angles, segments, rows, edge = thickness.shape
+    groups = starts.shape[1]
+    stages = groups.bit_length() - 1
+    blocks = order.shape[0]
+    chunks = math.gcd(chunk_total, blocks)
+    per_chunk = blocks // chunks
     smem = pl.BlockSpec(memory_space=pltpu.SMEM)
     vmem = pl.BlockSpec(memory_space=pltpu.VMEM)
-    flops = 2 * len(thick) * angles * blocks * rows * edge * edge
+    dma = pltpu.SemaphoreType.DMA
+    halves = [groups >> (stage + 1) for stage in range(stages)]
+    data = [pltpu.VMEM((chunks, per_chunk, half, capacity, edge), jnp.int16) for half in halves]
+    unit = [pltpu.VMEM((chunks, per_chunk * half, edge), jnp.float32) for half in halves]
     return pl.pallas_call(
-        functools.partial(backproject_kernel, first),
-        out_shape=jax.ShapeDtypeStruct((groups, blocks, capacity, edge), jnp.float32),
-        in_specs=[smem] * 5 + [vmem] * (len(thick) + 1),
+        functools.partial(reduce_kernel, stages, cores, chunks),
+        out_shape=jax.ShapeDtypeStruct((blocks, capacity, edge), jnp.float32),
+        in_specs=[smem] * 5 + [vmem] * 2,
         out_specs=vmem,
-        scratch_shapes=[pltpu.VMEM((unroll_blocks, rows + capacity, edge), jnp.float32)],
-        compiler_params=pltpu.CompilerParams(vmem_limit_bytes=32 * 2**20),
-        cost_estimate=pl.CostEstimate(
-            flops=flops, bytes_accessed=4 * groups * blocks * capacity * edge, transcendentals=0
+        scratch_shapes=[
+            pltpu.VMEM((cores - 1, angles, segments, rows, edge), jnp.bfloat16),
+            pltpu.VMEM((per_chunk, rows + capacity, edge), jnp.float32),
+            pltpu.VMEM((blocks, rows, edge), jnp.float32),
+            pltpu.VMEM((blocks, groups // 2, capacity, edge), jnp.float32),
+            dma((cores - 1, angles)),
+            dma((cores - 1, angles)),
+            dma((stages, chunks)),
+            dma((stages, chunks)),
+            dma((stages, chunks)),
+            dma((stages, chunks)),
+            *data, *data, *unit, *unit,
+        ],
+        compiler_params=pltpu.CompilerParams(
+            vmem_limit_bytes=40 * 2**20, collective_id=0, has_side_effects=True
         ),
-        name="backproject",
-    )(seg_rows, tile_rows, order, starts, counts, *thick, tiles)
-
-
-def butterfly(partial, scale, lead):
-    total = partial.shape[0]
-    bits = total.bit_length() - 1
-    remaining = list(range(bits - 1, -1, -1))
-    current = partial.reshape((2,) * bits + partial.shape[1:])
-    order = list(range(bits))
-    if bits > 1 and lead:
-        order[0], order[1] = order[1], order[0]
-    for bit in order:
-        axis = remaining.index(bit)
-        remaining.remove(bit)
-        keep = lax.index_in_dim(current, 0, axis, keepdims=False)
-        send = lax.index_in_dim(current, 1, axis, keepdims=False)
-        pairs = [(i, i ^ (1 << bit)) for i in range(total)]
-        came = lax.ppermute((send * scale).astype(link_type), "angle", pairs)
-        current = keep + came.astype(jnp.float32) / scale
-    return current
+        name="backproject_reduce",
+    )(seg_rows, tile_rows, order, starts, counts, thickness, tiles)
 
 
 def per_device(intensity, counts, segment_ids, tile_ids, block_order, tiles):
@@ -190,15 +321,11 @@
     core = lax.axis_index("tile")
     capacity = 2 * rows // groups
     blocks = block_order.shape[0] // cores
-    angle_total = segment_ids.shape[0]
 
     thickness = paganin_thickness(intensity, edge)
-    thick, angle_rows = [thickness], [(place * cores + core) * angles]
-    for step in range(1, cores):
-        pairs = [(i, (i + step) % cores) for i in range(cores)]
-        thick.append(lax.ppermute(thickness, "tile", pairs))
-        angle_rows.append((place * cores + (core - step) % cores) * angles)
-
+    angle_rows = [
+        (place * cores + (core - step) % cores) * angles for step in range(cores)
+    ]
     seg_rows = jnp.concatenate(
         [lax.dynamic_slice_in_dim(segment_ids, row, angles) for row in angle_rows]
     )
@@ -206,26 +333,26 @@
         [lax.dynamic_slice_in_dim(tile_ids, row, angles) for row in angle_rows]
     )
     order = lax.dynamic_slice_in_dim(block_order, core * blocks, blocks)
-    relative = jnp.arange(groups, dtype=jnp.int32)
-    member = relative[None, :] == (relative ^ place)[:, None]
-    before = relative[None, :] < (relative ^ place)[:, None]
-    near_counts = jnp.sum(jnp.where(member, counts[None, :], 0), axis=1)
-    near_starts = jnp.sum(jnp.where(before, counts[None, :], 0), axis=1)
-
-    largest = jnp.max(jnp.abs(tiles.astype(jnp.float32)))
-    bound = 1.75 * angle_total * edge * jnp.where(largest > 0.0, largest, 1.0)
-    scale = 60000.0 / bound
-
-    chunks = math.gcd(chunk_total, blocks)
-    per_chunk = blocks // chunks
-    finished = []
-    for c in range(chunks):
-        partial = backproject(
-            thick, seg_rows, tile_rows, order, near_starts, near_counts, tiles,
-            c * per_chunk, per_chunk, capacity,
-        )
-        finished.append(butterfly(partial, scale, c % 2))
-    volume = jnp.concatenate(finished, axis=0)
+
+    stages = groups.bit_length() - 1
+    bit_order = list(range(stages))
+    swapped = bit_order[:]
+    if stages > 1:
+        swapped[0], swapped[1] = 1, 0
+    offsets = np.array(
+        [
+            [sum(((p >> (stages - 1 - i)) & 1) << bits[i] for i in range(stages)) for p in range(groups)]
+            for bits in (bit_order, swapped)
+        ],
+        np.int32,
+    )
+    owner = jnp.asarray(offsets) ^ place
+    index = jnp.arange(groups, dtype=jnp.int32)
+    near_counts = jnp.sum(jnp.where(index == owner[..., None], counts, 0), axis=-1)
+    near_starts = jnp.sum(jnp.where(index < owner[..., None], counts, 0), axis=-1)
+    volume = reduced_blocks(
+        thickness, seg_rows, tile_rows, order, near_starts, near_counts, tiles, capacity, cores
+    )
     return jnp.swapaxes(volume, 0, 1)[None]
 
 

time: 54.6 us -> 57.9 us (1.060)
  Pallas kernels: 15.2 us -> 51.8 us
  starting transfers between devices: 17.8 us -> 0 us
  waiting for transfers between devices: 12.3 us -> 0 us
  other arithmetic: 4.69 us -> 1.56 us
  between operations: 1.57 us -> 0.02 us
  local copies, waits for them, and re-layouts: 2.73 us -> 4.26 us
    pallas_call x4 -> x1, Pallas kernels: 6.62 us -> 43.2 us  [reduced_blocks(): pl.pallas_call(functools.partial(reduce_kernel, stages, cores, chunks), o...]
    ppermute x13 -> x0, starting transfers between devices: 17.8 us -> none  [the longest x12 17.3 us: butterfly(): came = lax.ppermute((send * scale).astype(link_type), 'angle', pairs)]
    ppermute x13 -> x0, waiting for transfers between devices: 12.3 us -> none  [the longest x12 11.4 us: butterfly(): came = lax.ppermute((send * scale).astype(link_type), 'angle', pairs)]
    add x12 -> x0, other arithmetic: 1.54 us -> none  [butterfly(): current = keep + came.astype(jnp.float32) / scale]
    convert_element_type x12 -> x0, other arithmetic: 1.45 us -> none  [butterfly(): came = lax.ppermute((send * scale).astype(link_type), 'angle', pairs)]
    broadcast_in_dim x0 -> x1, local copies, waits for them, and re-layouts: none -> 1.1 us  [per_device(): return jnp.swapaxes(volume, 0, 1)[None]]
    broadcast_in_dim x1 -> x0, other arithmetic: 0.83 us -> none  [per_device(): return jnp.swapaxes(volume, 0, 1)[None]]
    dynamic_slice x1, local copies, waits for them, and re-layouts: 0.08 us -> 0.79 us  [per_device(): order = lax.dynamic_slice_in_dim(block_order, core * blocks, blocks)]
  transfers between devices with their start and end apart: 13 -> 0, of which waited for: 6 -> 0; matrix products, arithmetic and copies ran while one was open for 8% -> 0% of each run, Pallas kernels for 9% -> 0%
where the time goes in v2:
time: 57.9 us; the launch traced here: 57.6 us
  Pallas kernels  51.8 us (89%)
  local copies, waits for them, and re-layouts  4.26 us (7%)
  other arithmetic  1.56 us (3%)
    pallas_call x1, Pallas kernels, reduced_blocks(): pl.pallas_call(functools.partial(reduce_kernel, stages, cores, chunks), o...  43.2 us
    pallas_call x1, Pallas kernels, paganin_thickness(): pl.pallas_call(filter_kernel, grid=(angles,), out_shape=jax.ShapeDtypeStr...  8.59 us
    unnamed x4, local copies, waits for them, and re-layouts  1.59 us

profile of v2, /device:TPU:0, one launch (start us, length us, event | category | flops | bytes accessed | tf_op | source)
XLA Modules:
  0.0 57.6 jit_solution(7405474645817367225)
XLA Ops:
  0.0 0.0 copy-start.1
  0.0 0.8 %dynamic_slice.19.order_ref = s32[32]{0:T(128)S(1)} dynamic-slice(s32[64]{0:T(128)} %param.14, s32[]{:T(128)S(6)} %select_n.33), dynamic_slice_sizes={32} | dynamic-slice | bytes 260 | tf_op jit(solution)/shard_map/dynamic_slice | solution.py:335
  0.8 0.7 %broadcast_xor_fusion = s32[2,8]{1,0:T(2,128)S(1)} fusion(s32[2,8]{1,0:T(2,128)} %constant.46.clone, s32[]{:T(128)S(6)} %axis_index.23), kind=kLoop, calls=%fused_computation.10 | loop fusion | flops 16 | bytes 132 | tf_op jit(solution)/shard_map/xor | solution.py:349
  1.5 0.9 %select_reduce_fusion = (s32[2,8]{1,0:T(2,128)S(1)}, s32[2,8]{1,0:T(2,128)S(1)}) fusion(s32[8]{0:T(128)} %param.11, s32[2,8]{1,0:T(2,128)S(1)} %broadcast_xor_fusion), kind=kLoop, calls=%fused_computation | loop fusion | flops 736 | bytes 224 | tf_op jit(solution)/shard_map/reduce_sum | solution.py:351
  2.3 0.8 %constant_dynamic-slice_fusion.1 = (s32[4,64]{1,0:T(4,128)S(1)}, s32[4,64]{1,0:T(4,128)S(1)}, s32[4,64]{1,0:T(4,128)S(1)}, s32[4,64]{1,0:T(4,128)S(1)}) fusion(s32[64,64]{1,0:T(8,128)} %param.13, s32[]{:T(128)S(6)} %select_n.30, s32[]{:T(128)S(6)} %select_n.32, s32[64,64]{1,0:T(8,128)} %param.12), kind=kLoop, calls=%fused_computation.7 | loop fusion | bytes 8200 | tf_op jit(solution)/shard_map/dynamic_slice | solution.py:333
  3.1 8.6 %paganin_filter.1.own = bf16[4,16,128,128]{3,2,1,0:T(8,128)(2,1)} custom-call(f32[4,128,2048]{2,1,0:T(8,128)} %x_ref.1, bf16[256,256]{1,0:T(8,128)(2,1)} %constant.43.clone.forward_ref, bf16[256,256]{1,0:T(8,128)(2,1)} %constant.44.clone.inverse_ref, f32[256,128]{1,0:T(8,128)} %constant.45.clone.power_ref), custom_call_target="tpu_custom_call" | custom-call | tf_op jit(solution)/shard_map/paganin_filter/pallas_call | solution.py:99
  11.7 0.0 copy-done.1
  11.7 0.0 copy-start
  11.7 1.6 %copy-done = bf16[4,16,128,128]{3,2,1,0:T(8,128)(2,1)S(1)} copy-done((bf16[4,16,128,128]{3,2,1,0:T(8,128)(2,1)S(1)}, bf16[4,16,128,128]{3,2,1,0:T(8,128)(2,1)}, u32[]{:S(2)}) %copy-start) | copy-done | bytes 2097176
  13.3 43.2 %backproject_reduce.1 = f32[32,32,128]{2,1,0:T(8,128)S(1)} custom-call(s32[8,64]{1,0:T(8,128)S(1)} %pad_add_fusion.seg_ref, s32[8,64]{1,0:T(8,128)S(1)} %pad_add_fusion.1.tile_ref, s32[32]{0:T(128)S(1)} %dynamic_slice.19.order_ref, s32[2,8]{1,0:T(2,128)S(1)} %get-tuple-element.6.start_ref, s32[2,8]{1,0:T(2,128)S(1)} %get-tuple-element.5.count_ref, ...), custom_call_target="tpu_custom_call" | custom-call | tf_op jit(solution)/shard_map/backproject_reduce/pallas_call | solution.py:290
  56.5 1.1 %copy.12 = f32[1,32,32,128]{3,2,1,0:T(8,128)} copy(f32[1,32,32,128]{3,1,2,0:T(8,128)S(1)} %bitcast.3) | data formatting | bytes 1048576 | tf_op jit(solution)/shard_map/broadcast_in_dim | solution.py:356
  (2 shorter events, 0.0 us)
Async XLA Ops:
  0.0 11.7 %copy-start.1 = (bf16[16,128,128]{2,1,0:T(8,128)(2,1)S(1)}, bf16[16,128,128]{2,1,0:T(8,128)(2,1)}, u32[]{:S(2)}) copy-start(bf16[16,128,128]{2,1,0:T(8,128)(2,1)} %tiles_ref.1) | copy-start | bytes 1572868
  11.7 1.6 %copy-start = (bf16[4,16,128,128]{3,2,1,0:T(8,128)(2,1)S(1)}, bf16[4,16,128,128]{3,2,1,0:T(8,128)(2,1)}, u32[]{:S(2)}) copy-start(bf16[4,16,128,128]{3,2,1,0:T(8,128)(2,1)} %paganin_filter.1.own) | copy-start | bytes 6291460

commit v3 on v2

v3 whole, which is shorter than its diff:
```python
import functools
import math

import jax
import jax.numpy as jnp
import numpy as np
from jax import lax
from jax.experimental import pallas as pl
from jax.experimental.pallas import tpu as pltpu
from jax.sharding import PartitionSpec as P

paganin_alpha = 2.0
chunk_total = 16
lag = 3
code_top = 32760.0
round_shift = 12582912.0
MESH = pl.DeviceIdType.MESH
pitch_extra = 9


def split_pair(array):
    high = array.astype(jnp.bfloat16)
    low = (array - high.astype(jnp.float32)).astype(jnp.bfloat16)
    return high, low


def filter_tables(row_total, edge):
    index = np.arange(row_total)
    phase = 2.0 * np.pi * (index[:, None] * index[None, :] % row_total) / row_total
    hartley = (np.cos(phase) + np.sin(phase)) / math.sqrt(row_total)
    a = 1.0 + paganin_alpha * (4.0 * np.sin(np.pi * index / row_total) ** 2 + 2.0)
    pole = (a - np.sqrt(a * a - 4.0 * paganin_alpha**2)) / (2.0 * paganin_alpha)
    gain = pole / (paganin_alpha * (1.0 - pole * pole))

    def halves(matrix):
        high = matrix.astype(np.float32).astype(jnp.bfloat16)
        return high, (matrix - high.astype(np.float64)).astype(np.float32).astype(jnp.bfloat16)

    high, low = halves(hartley * gain[None, :])
    forward = np.concatenate([np.concatenate([high, low], 1)] * 2, 0)
    high, low = halves(hartley)
    inverse = np.concatenate([np.concatenate([high, high], 1), np.concatenate([low, low], 1)], 0)
    reach = pole[None, :] ** np.arange(1, edge + 1)[:, None]
    powers = np.concatenate([reach, reach[::-1]], 0).astype(np.float32)
    return forward, inverse, powers


def filter_one(x_ref, forward_ref, inverse_ref, power_ref, out_ref, spectrum, ahead_ref, behind_ref, ends):
    segments, rows, edge = out_ref.shape
    pitch = edge + pitch_extra
    for s in range(segments):
        high, low = split_pair(x_ref[:, s * edge : (s + 1) * edge])
        both = jnp.concatenate([high, low], axis=0)
        product = lax.dot_general(
            both, forward_ref[...], (((0,), (0,)), ((), ())), preferred_element_type=jnp.float32
        )
        spectrum[s * pitch : s * pitch + edge, :] = product[:, :rows] + product[:, rows:]
    pole = jnp.broadcast_to(power_ref[0:1, :], (segments, rows))
    zero = jnp.zeros((segments, rows), jnp.float32)

    def column(t):
        return pl.ds(t, segments, stride=pitch)

    def sweep(t, state):
        ahead, behind = state
        ahead = ahead * pole + spectrum[column(t), :]
        ahead_ref[column(t), :] = ahead
        back = edge - 1 - t
        behind = behind * pole
        behind_ref[column(back), :] = behind
        return ahead, behind + spectrum[column(back), :]

    ahead, behind = lax.fori_loop(0, edge, sweep, (zero, zero), unroll=16)
    ends[0] = ahead
    ends[1] = behind
    for s in range(segments):
        span = slice(s * pitch, s * pitch + edge)
        before, after = (s - 1) % segments, (s + 1) % segments
        value = ahead_ref[span, :] + behind_ref[span, :]
        value = value + power_ref[:edge, :] * ends[0, before : before + 1, :]
        value = value + power_ref[edge:, :] * ends[1, after : after + 1, :]
        high, low = split_pair(value)
        both = jnp.concatenate([high, low], axis=1)
        product = lax.dot_general(
            inverse_ref[...], both, (((1,), (1,)), ((), ())), preferred_element_type=jnp.float32
        )
        out_ref[s] = (-jnp.log(product[:rows] + product[rows:])).astype(jnp.bfloat16)


def encode(value):
    top = jnp.maximum(jnp.max(jnp.abs(value), axis=0, keepdims=True), 1e-30)
    scaled = value * (code_top / top)
    code = (scaled + round_shift) - round_shift
    return code.astype(jnp.int32).astype(jnp.int16), top * (1.0 / code_top)


def decode(code, unit):
    return code.astype(jnp.int32).astype(jnp.float32) * unit


def whole_kernel(
    stages, cores, chunks, count_ref, seg_ref, tile_ref, order_ref, x_hbm, forward_hbm, inverse_hbm,
    power_hbm, tiles_hbm, out_ref, x_buf, forward_ref, inverse_ref, power_ref, tiles_ref, spectrum,
    ahead_ref, behind_ref, ends, own, other, start_ref, rows_ref, kept, x_sem, load_sem, swap_send,
    swap_recv, data_send, data_recv, unit_send, unit_recv, *buffers
):
    send, came, send_unit, came_unit = (buffers[i * stages : (i + 1) * stages] for i in range(4))
    groups = 2**stages
    angles, _, rows, edge = own.shape
    blocks, capacity, _ = out_ref.shape
    per_chunk = blocks // chunks
    place, core = lax.axis_index("angle"), lax.axis_index("tile")

    loads = [
        pltpu.make_async_copy(source, target, load_sem.at[i])
        for i, (source, target) in enumerate(
            (
                (forward_hbm, forward_ref),
                (power_hbm, power_ref),
                (inverse_hbm, inverse_ref),
                (tiles_hbm, tiles_ref),
            )
        )
    ]

    def projection(a):
        return pltpu.make_async_copy(x_hbm.at[a], x_buf.at[a], x_sem.at[a])

    projection(0).start()
    for load in loads[:3]:
        load.start()
    for a in range(1, angles):
        projection(a).start()
    loads[3].start()

    def across(bit):
        return place + (1 - 2 * ((place // (1 << bit)) % 2)) * (1 << bit)

    partners = [across(bit) for bit in range(stages)]
    neighbours = [lax.rem(core + step, cores) for step in range(1, cores)]
    barrier = pltpu.get_barrier_semaphore()
    for partner in partners:
        pl.semaphore_signal(barrier, inc=1, device_id={"angle": partner}, device_id_type=MESH)
    for neighbour in neighbours:
        pl.semaphore_signal(barrier, inc=1, device_id={"tile": neighbour}, device_id_type=MESH)

    running = jnp.int32(0)
    for g in range(groups):
        start_ref[g] = running
        running = running + count_ref[g]
    for lane in range(per_chunk):
        rows_ref[lane, rows:, :] = jnp.zeros((capacity, edge), jnp.float32)
    for load in loads[:3]:
        load.wait()

    def swap(index, a):
        return pltpu.make_async_remote_copy(
            src_ref=own.at[a],
            dst_ref=other.at[index, a],
            send_sem=swap_send.at[index, a],
            recv_sem=swap_recv.at[index, a],
            device_id={"tile": neighbours[index]},
            device_id_type=MESH,
        )

    def filter_angle(a, _):
        projection(a).wait()
        filter_one(
            x_buf.at[a], forward_ref, inverse_ref, power_ref, own.at[a],
            spectrum, ahead_ref, behind_ref, ends,
        )

        @pl.when(a == 0)
        def _():
            pl.semaphore_wait(barrier, stages + cores - 1)

        for index in range(cores - 1):
            swap(index, a).start()
        return 0

    lax.fori_loop(0, angles, filter_angle, 0)
    loads[3].wait()
    for index in range(cores - 1):
        for a in range(angles):
            swap(index, a).wait()

    slot = lax.broadcasted_iota(jnp.int32, (capacity, edge), 0)
    thick_rows = [(lambda a, s: own[a, s], (place * cores + core) * angles)]
    for index in range(cores - 1):
        source = lax.rem(core + cores - 1 - index, cores)
        thick_rows.append(
            (lambda a, s, index=index: other[index, a, s], (place * cores + source) * angles)
        )

    def project(v):
        block = order_ref[core * blocks + v]
        pieces, maps = [], []
        for thick, first_row in thick_rows:
            for a in range(angles):
                pieces.append(thick(a, seg_ref[first_row + a, block]))
                maps.append(tiles_ref[tile_ref[first_row + a, block]])
        return jnp.dot(
            jnp.concatenate(pieces, axis=1),
            jnp.concatenate(maps, axis=0),
            preferred_element_type=jnp.float32,
        )

    def variant_of(c):
        return ((c + 2) % 4) // 3 if stages > 1 else 0

    def owner(variant, position):
        group = place
        for i in range(stages):
            if (position >> (stages - 1 - i)) & 1:
                move = partners[i] - place
                if stages > 1 and i < 2:
                    move = move * (1 - variant) + (partners[1 - i] - place) * variant
                group = group + move
        return group

    def copies(stage, c):
        partner = partners[stage]
        if stages > 1 and stage < 2:
            variant = variant_of(c)
            partner = partners[stage] * (1 - variant) + partners[1 - stage] * variant
        made = []
        for source, target, sent, got in (
            (send[stage], came[stage], data_send, data_recv),
            (send_unit[stage], came_unit[stage], unit_send, unit_recv),
        ):
            made.append(
                pltpu.make_async_remote_copy(
                    src_ref=source.at[c],
                    dst_ref=target.at[c],
                    send_sem=sent.at[stage, c],
                    recv_sem=got.at[stage, c],
                    device_id={"angle": partner},
                    device_id_type=MESH,
                )
            )
        return made

    def ship(stage, c, lane, position, value):
        half = groups >> (stage + 1)
        code, unit = encode(value)
        send[stage][c, lane, position - half] = code
        send_unit[stage][c, lane * half + position - half : lane * half + position - half + 1, :] = unit

    def begin(c):
        variant = variant_of(c)
        for lane in range(per_chunk):
            v = c * per_chunk + lane
            rows_ref[lane, :rows, :] = project(v)
        for g in range(groups):
            group = owner(variant, g)
            start, count = start_ref[group], count_ref[group]
            for lane in range(per_chunk):
                v = c * per_chunk + lane
                picked = rows_ref[lane, pl.ds(start, capacity), :]
                picked = jnp.where(slot < count, picked, 0.0)
                if g < groups // 2:
                    kept[v, g] = picked
                else:
                    ship(0, c, lane, g, picked)
        for copy in copies(0, c):
            copy.start()

    def advance(stage, c):
        for copy in copies(stage - 1, c):
            copy.wait()
        left = groups >> stage
        for lane in range(per_chunk):
            v = c * per_chunk + lane
            for g in range(left):
                unit = came_unit[stage - 1][c, lane * left + g : lane * left + g + 1, :]
                value = kept[v, g] + decode(came[stage - 1][c, lane, g], unit)
                if stage == stages:
                    out_ref[v] = value
                elif g < left // 2:
                    kept[v, g] = value
                else:
                    ship(stage, c, lane, g, value)
        if stage < stages:
            for copy in copies(stage, c):
                copy.start()

    def step_body(step, _):
        @pl.when(step < chunks)
        def _():
            begin(step)

        for stage in range(stages, 0, -1):
            c = step - stage * lag

            @pl.when((c >= 0) & (c < chunks))
            def _(stage=stage, c=c):
                advance(stage, c)

        return 0

    lax.fori_loop(0, chunks + stages * lag, step_body, 0)


def per_device(intensity, counts, segment_ids, tile_ids, block_order, tiles):
    angles, rows, width = intensity.shape
    edge = tiles.shape[1]
    segments = width // edge
    groups = lax.axis_size("angle")
    cores = lax.axis_size("tile")
    stages = groups.bit_length() - 1
    capacity = 2 * rows // groups
    blocks = block_order.shape[0] // cores
    chunks = math.gcd(chunk_total, blocks)
    per_chunk = blocks // chunks
    forward, inverse, powers = filter_tables(rows, edge)

    smem = pl.BlockSpec(memory_space=pltpu.SMEM)
    vmem = pl.BlockSpec(memory_space=pltpu.VMEM)
    hbm = pl.BlockSpec(memory_space=pl.ANY)
    dma = pltpu.SemaphoreType.DMA
    f32, bf16 = jnp.float32, jnp.bfloat16
    plane = pltpu.VMEM((segments * (edge + pitch_extra), rows), f32)
    halves = [groups >> (stage + 1) for stage in range(stages)]
    data = [pltpu.VMEM((chunks, per_chunk, half, capacity, edge), jnp.int16) for half in halves]
    unit = [pltpu.VMEM((chunks, per_chunk * half, edge), f32) for half in halves]
    volume = pl.pallas_call(
        functools.partial(whole_kernel, stages, cores, chunks),
        out_shape=jax.ShapeDtypeStruct((blocks, capacity, edge), f32),
        in_specs=[smem] * 4 + [hbm] * 5,
        out_specs=vmem,
        scratch_shapes=[
            pltpu.VMEM(intensity.shape, f32),
            pltpu.VMEM(forward.shape, bf16),
            pltpu.VMEM(inverse.shape, bf16),
            pltpu.VMEM(powers.shape, f32),
            pltpu.VMEM(tiles.shape, bf16),
            plane, plane, plane,
            pltpu.VMEM((2, segments, rows), f32),
            pltpu.VMEM((angles, segments, rows, edge), bf16),
            pltpu.VMEM((cores - 1, angles, segments, rows, edge), bf16),
            pltpu.SMEM((groups,), jnp.int32),
            pltpu.VMEM((per_chunk, rows + capacity, edge), f32),
            pltpu.VMEM((blocks, groups // 2, capacity, edge), f32),
            dma((angles,)),
            dma((4,)),
            dma((cores - 1, angles)),
            dma((cores - 1, angles)),
            dma((stages, chunks)),
            dma((stages, chunks)),
            dma((stages, chunks)),
            dma((stages, chunks)),
            *data, *data, *unit, *unit,
        ],
        compiler_params=pltpu.CompilerParams(
            vmem_limit_bytes=60 * 2**20, collective_id=0, has_side_effects=True
        ),
        name="tomography",
    )(
        counts, segment_ids, tile_ids, block_order, intensity,
        jnp.asarray(forward), jnp.asarray(inverse), jnp.asarray(powers), tiles,
    )
    return jnp.swapaxes(volume, 0, 1)[None]


def solution(mesh):
    in_specs = (P(("groups", "angle", "tile"), None, None), P("groups"), P(), P(), P("groups"), P())
    out_specs = P(("groups", "angle"), None, "tile", None)
    return jax.shard_map(
        per_device, mesh=mesh, in_specs=in_specs, out_specs=out_specs, check_vma=False
    )
```

time: 57.9 us -> 50.2 us (0.87)
  Pallas kernels: 51.8 us -> 47.7 us
  local copies, waits for them, and re-layouts: 4.26 us -> 2.14 us
  other arithmetic: 1.56 us -> 0 us
    pallas_call x2 -> x1, Pallas kernels: 51.8 us -> 47.7 us  [per_device(): pl.pallas_call(functools.partial(whole_kernel, stages, cores, chunks), ou...]
    unnamed x4 -> x0, local copies, waits for them, and re-layouts: 1.59 us -> none
    dynamic_slice x2 -> x0, local copies, waits for them, and re-layouts: 1.57 us -> none  [the longest x1 0.79 us: per_device(): order = lax.dynamic_slice_in_dim(block_order, core * blocks, blocks)]
    broadcast_in_dim x1, local copies, waits for them, and re-layouts: 1.1 us -> 2.14 us  [per_device(): return jnp.swapaxes(volume, 0, 1)[None]]
    reduce_sum x1 -> x0, other arithmetic: 0.86 us -> none  [per_device(): jnp.sum(jnp.where(index == owner[..., None], counts, 0), axis=-1)]
    xor x1 -> x0, other arithmetic: 0.68 us -> none  [per_device(): owner = jnp.asarray(offsets) ^ place]
where the time goes in v3:
time: 50.2 us; the launch traced here: 49.9 us
  Pallas kernels  47.7 us (95%)
  local copies, waits for them, and re-layouts  2.14 us (4%)
    pallas_call x1, Pallas kernels, per_device(): pl.pallas_call(functools.partial(whole_kernel, stages, cores, chunks), ou...  47.7 us
    broadcast_in_dim x1, local copies, waits for them, and re-layouts, per_device(): return jnp.swapaxes(volume, 0, 1)[None]  2.14 us

profile of v3, /device:TPU:0, one launch (start us, length us, event | category | flops | bytes accessed | tf_op | source)
XLA Modules:
  0.0 49.9 jit_solution(18238507677531662518)
XLA Ops:
  0.0 47.7 %tomography.1 = f32[32,32,128]{2,1,0:T(8,128)} custom-call(s32[8]{0:T(128)} %count_ref.1, s32[64,64]{1,0:T(8,128)} %seg_ref.1, s32[64,64]{1,0:T(8,128)} %tile_ref.1, s32[64]{0:T(128)} %order_ref.1, f32[4,128,2048]{2,1,0:T(8,128)} %x_hbm.1, bf16[256,256]{1,0:T(8,128)(2,1)} %constant.6.clone.forward_hbm, bf16[256,256]{1,0:T(8,128)(2,1)} %constant.7.clone.inverse_hbm, ...), custom_call_target="tpu_custom_call" | custom-call | tf_op jit(solution)/shard_map/tomography/pallas_call | solution.py:326
  47.7 2.1 %copy.10 = f32[1,32,32,128]{3,2,1,0:T(8,128)} copy(f32[1,32,32,128]{3,1,2,0:T(8,128)} %bitcast.3) | data formatting | bytes 1048576 | tf_op jit(solution)/shard_map/broadcast_in_dim | solution.py:362

commit v4 on v3

--- a/solution.py
+++ b/solution.py
@@ -10,7 +10,8 @@
 from jax.sharding import PartitionSpec as P
 
 paganin_alpha = 2.0
-chunk_total = 16
+chunk_total = 8
+sublanes = 8
 lag = 3
 code_top = 32760.0
 round_shift = 12582912.0
@@ -107,7 +108,7 @@
     send, came, send_unit, came_unit = (buffers[i * stages : (i + 1) * stages] for i in range(4))
     groups = 2**stages
     angles, _, rows, edge = own.shape
-    blocks, capacity, _ = out_ref.shape
+    capacity, blocks, _ = out_ref.shape
     per_chunk = blocks // chunks
     place, core = lax.axis_index("angle"), lax.axis_index("tile")
 
@@ -206,7 +207,7 @@
         )
 
     def variant_of(c):
-        return ((c + 2) % 4) // 3 if stages > 1 else 0
+        return (c + 1) % 2 if stages > 1 else 0
 
     def owner(variant, position):
         group = place
@@ -240,49 +241,59 @@
             )
         return made
 
-    def ship(stage, c, lane, position, value):
+    def ship(stage, c, tiles_out):
         half = groups >> (stage + 1)
-        code, unit = encode(value)
-        send[stage][c, lane, position - half] = code
-        send_unit[stage][c, lane * half + position - half : lane * half + position - half + 1, :] = unit
+        coded = [(lane, g, *encode(value)) for lane, g, value in tiles_out]
+        for lane, g, code, unit in coded:
+            row = lane * half + g - half
+            send[stage][c, lane, g - half] = code
+            send_unit[stage][c, row : row + 1, :] = unit
 
     def begin(c):
         variant = variant_of(c)
         for lane in range(per_chunk):
-            v = c * per_chunk + lane
-            rows_ref[lane, :rows, :] = project(v)
-        for g in range(groups):
-            group = owner(variant, g)
-            start, count = start_ref[group], count_ref[group]
-            for lane in range(per_chunk):
-                v = c * per_chunk + lane
-                picked = rows_ref[lane, pl.ds(start, capacity), :]
-                picked = jnp.where(slot < count, picked, 0.0)
-                if g < groups // 2:
-                    kept[v, g] = picked
-                else:
-                    ship(0, c, lane, g, picked)
+            rows_ref[lane, :rows, :] = project(c * per_chunk + lane)
+        spans = [owner(variant, g) for g in range(groups)]
+        spans = [(start_ref[group], slot < count_ref[group]) for group in spans]
+
+        def picked(lane, g):
+            start, inside = spans[g]
+            return jnp.where(inside, rows_ref[lane, pl.ds(start, capacity), :], 0.0)
+
+        for lane in range(per_chunk):
+            ship(0, c, [(lane, g, picked(lane, g)) for g in range(groups // 2, groups)])
         for copy in copies(0, c):
             copy.start()
+        for lane in range(per_chunk):
+            held = [picked(lane, g) for g in range(groups // 2)]
+            for g, value in enumerate(held):
+                kept[c * per_chunk + lane, g] = value
 
     def advance(stage, c):
         for copy in copies(stage - 1, c):
             copy.wait()
         left = groups >> stage
-        for lane in range(per_chunk):
-            v = c * per_chunk + lane
-            for g in range(left):
-                unit = came_unit[stage - 1][c, lane * left + g : lane * left + g + 1, :]
-                value = kept[v, g] + decode(came[stage - 1][c, lane, g], unit)
-                if stage == stages:
-                    out_ref[v] = value
-                elif g < left // 2:
-                    kept[v, g] = value
-                else:
-                    ship(stage, c, lane, g, value)
-        if stage < stages:
-            for copy in copies(stage, c):
-                copy.start()
+
+        def value(lane, g):
+            unit = came_unit[stage - 1][c, lane * left + g : lane * left + g + 1, :]
+            return kept[c * per_chunk + lane, g] + decode(came[stage - 1][c, lane, g], unit)
+
+        if stage == stages:
+            for lane, last in enumerate([value(lane, 0) for lane in range(per_chunk)]):
+                kept[c * per_chunk + lane, 0] = last
+            return
+        half = left // 2
+        lanes_at_once = max(1, 4 // half)
+        for first in range(0, per_chunk, lanes_at_once):
+            lanes = range(first, min(per_chunk, first + lanes_at_once))
+            ship(stage, c, [(lane, g, value(lane, g)) for lane in lanes for g in range(half, left)])
+        for copy in copies(stage, c):
+            copy.start()
+        for first in range(0, per_chunk, lanes_at_once):
+            lanes = range(first, min(per_chunk, first + lanes_at_once))
+            held = [(lane, g, value(lane, g)) for lane in lanes for g in range(half)]
+            for lane, g, tile in held:
+                kept[c * per_chunk + lane, g] = tile
 
     def step_body(step, _):
         @pl.when(step < chunks)
@@ -299,6 +310,8 @@
         return 0
 
     lax.fori_loop(0, chunks + stages * lag, step_body, 0)
+    for v in range(0, blocks, sublanes):
+        out_ref[:, v : v + sublanes, :] = jnp.swapaxes(kept[v : v + sublanes, 0], 0, 1)
 
 
 def per_device(intensity, counts, segment_ids, tile_ids, block_order, tiles):
@@ -325,7 +338,7 @@
     unit = [pltpu.VMEM((chunks, per_chunk * half, edge), f32) for half in halves]
     volume = pl.pallas_call(
         functools.partial(whole_kernel, stages, cores, chunks),
-        out_shape=jax.ShapeDtypeStruct((blocks, capacity, edge), f32),
+        out_shape=jax.ShapeDtypeStruct((capacity, blocks, edge), f32),
         in_specs=[smem] * 4 + [hbm] * 5,
         out_specs=vmem,
         scratch_shapes=[
@@ -359,7 +372,7 @@
         counts, segment_ids, tile_ids, block_order, intensity,
         jnp.asarray(forward), jnp.asarray(inverse), jnp.asarray(powers), tiles,
     )
-    return jnp.swapaxes(volume, 0, 1)[None]
+    return volume[None]
 
 
 def solution(mesh):

time: 50.2 us -> 47.7 us (0.950)
  Pallas kernels: 47.7 us -> 45.5 us
    pallas_call x1, Pallas kernels: 47.7 us -> 45.5 us  [per_device(): pl.pallas_call(functools.partial(whole_kernel, stages, cores, chunks), ou...]
    broadcast_in_dim x1 -> x0, local copies, waits for them, and re-layouts: 2.14 us -> none  [per_device(): return jnp.swapaxes(volume, 0, 1)[None]]
    unnamed x0 -> x1, local copies, waits for them, and re-layouts: none -> 1.87 us
where the time goes in v4:
time: 47.7 us; the launch traced here: 47.4 us
  Pallas kernels  45.5 us (95%)
  local copies, waits for them, and re-layouts  1.87 us (4%)
    pallas_call x1, Pallas kernels, per_device(): pl.pallas_call(functools.partial(whole_kernel, stages, cores, chunks), ou...  45.5 us
    unnamed x1, local copies, waits for them, and re-layouts  1.87 us

profile of v4, /device:TPU:0, one launch (start us, length us, event | category | flops | bytes accessed | tf_op | source)
XLA Modules:
  0.0 47.4 jit_solution(3077134496000170639)
XLA Ops:
  0.0 45.5 %tomography.1 = f32[32,32,128]{2,1,0:T(8,128)} custom-call(s32[8]{0:T(128)} %count_ref.1, s32[64,64]{1,0:T(8,128)} %seg_ref.1, s32[64,64]{1,0:T(8,128)} %tile_ref.1, s32[64]{0:T(128)} %order_ref.1, f32[4,128,2048]{2,1,0:T(8,128)} %x_hbm.1, bf16[256,256]{1,0:T(8,128)(2,1)} %constant.6.clone.forward_hbm, bf16[256,256]{1,0:T(8,128)(2,1)} %constant.7.clone.inverse_hbm, ...), custom_call_target="tpu_custom_call" | custom-call | tf_op jit(solution)/shard_map/tomography/pallas_call | solution.py:339
  45.5 1.9 %copy.11 = f32[1,32,32,128]{3,2,1,0:T(8,128)} copy(f32[1,32,32,128]{3,2,1,0:T(8,128)} %bitcast.1) | data formatting | bytes 1048576

commit v5 on v4

--- a/solution.py
+++ b/solution.py
@@ -10,9 +10,9 @@
 from jax.sharding import PartitionSpec as P
 
 paganin_alpha = 2.0
-chunk_total = 8
+chunk_total = 16
 sublanes = 8
-lag = 3
+lag = 4
 code_top = 32760.0
 round_shift = 12582912.0
 MESH = pl.DeviceIdType.MESH
@@ -46,8 +46,9 @@
     return forward, inverse, powers
 
 
-def filter_one(x_ref, forward_ref, inverse_ref, power_ref, out_ref, spectrum, ahead_ref, behind_ref, ends):
-    segments, rows, edge = out_ref.shape
+def spread(x_ref, forward_ref, spectrum, segments):
+    rows, width = x_ref.shape
+    edge = width // segments
     pitch = edge + pitch_extra
     for s in range(segments):
         high, low = split_pair(x_ref[:, s * edge : (s + 1) * edge])
@@ -56,24 +57,39 @@
             both, forward_ref[...], (((0,), (0,)), ((), ())), preferred_element_type=jnp.float32
         )
         spectrum[s * pitch : s * pitch + edge, :] = product[:, :rows] + product[:, rows:]
+
+
+def sweep_columns(power_ref, planes, ends, segments, edge):
+    rows = power_ref.shape[1]
     pole = jnp.broadcast_to(power_ref[0:1, :], (segments, rows))
     zero = jnp.zeros((segments, rows), jnp.float32)
 
     def column(t):
-        return pl.ds(t, segments, stride=pitch)
-
-    def sweep(t, state):
-        ahead, behind = state
-        ahead = ahead * pole + spectrum[column(t), :]
-        ahead_ref[column(t), :] = ahead
+        return pl.ds(t, segments, stride=edge + pitch_extra)
+
+    def sweep(t, states):
         back = edge - 1 - t
-        behind = behind * pole
-        behind_ref[column(back), :] = behind
-        return ahead, behind + spectrum[column(back), :]
-
-    ahead, behind = lax.fori_loop(0, edge, sweep, (zero, zero), unroll=16)
-    ends[0] = ahead
-    ends[1] = behind
+        inputs = [
+            (spectrum[column(t), :], spectrum[column(back), :]) for spectrum, _, _ in planes
+        ]
+        following = []
+        for (_, ahead_ref, behind_ref), (x, y), (ahead, behind) in zip(planes, inputs, states):
+            ahead = ahead * pole + x
+            behind = behind * pole
+            ahead_ref[column(t), :] = ahead
+            behind_ref[column(back), :] = behind
+            following.append((ahead, behind + y))
+        return following
+
+    states = lax.fori_loop(0, edge, sweep, [(zero, zero) for _ in planes], unroll=8)
+    for k, (ahead, behind) in enumerate(states):
+        ends[k, 0] = ahead
+        ends[k, 1] = behind
+
+
+def finish(inverse_ref, power_ref, ahead_ref, behind_ref, ends, out_ref):
+    segments, rows, edge = out_ref.shape
+    pitch = edge + pitch_extra
     for s in range(segments):
         span = slice(s * pitch, s * pitch + edge)
         before, after = (s - 1) % segments, (s + 1) % segments
@@ -110,6 +126,7 @@
     angles, _, rows, edge = own.shape
     capacity, blocks, _ = out_ref.shape
     per_chunk = blocks // chunks
+    together = spectrum.shape[0]
     place, core = lax.axis_index("angle"), lax.axis_index("tile")
 
     loads = [
@@ -149,7 +166,8 @@
     for g in range(groups):
         start_ref[g] = running
         running = running + count_ref[g]
-    for lane in range(per_chunk):
+    begin_chunks = rows_ref.shape[0] // per_chunk
+    for lane in range(begin_chunks * per_chunk):
         rows_ref[lane, rows:, :] = jnp.zeros((capacity, edge), jnp.float32)
     for load in loads[:3]:
         load.wait()
@@ -164,22 +182,26 @@
             device_id_type=MESH,
         )
 
-    def filter_angle(a, _):
-        projection(a).wait()
-        filter_one(
-            x_buf.at[a], forward_ref, inverse_ref, power_ref, own.at[a],
-            spectrum, ahead_ref, behind_ref, ends,
-        )
-
-        @pl.when(a == 0)
-        def _():
-            pl.semaphore_wait(barrier, stages + cores - 1)
-
-        for index in range(cores - 1):
-            swap(index, a).start()
+    def filter_angles(step, _):
+        planes = [(spectrum.at[k], ahead_ref.at[k], behind_ref.at[k]) for k in range(together)]
+        for k in range(together):
+            projection(step * together + k).wait()
+            spread(x_buf.at[step * together + k], forward_ref, spectrum.at[k], own.shape[1])
+        sweep_columns(power_ref, planes, ends, own.shape[1], edge)
+        for k in range(together):
+            a = step * together + k
+            finish(inverse_ref, power_ref, ahead_ref.at[k], behind_ref.at[k], ends.at[k], own.at[a])
+            if k == 0:
+
+                @pl.when(step == 0)
+                def _():
+                    pl.semaphore_wait(barrier, stages + cores - 1)
+
+            for index in range(cores - 1):
+                swap(index, a).start()
         return 0
 
-    lax.fori_loop(0, angles, filter_angle, 0)
+    lax.fori_loop(0, angles // together, filter_angles, 0)
     loads[3].wait()
     for index in range(cores - 1):
         for a in range(angles):
@@ -249,25 +271,27 @@
             send[stage][c, lane, g - half] = code
             send_unit[stage][c, row : row + 1, :] = unit
 
-    def begin(c):
-        variant = variant_of(c)
-        for lane in range(per_chunk):
-            rows_ref[lane, :rows, :] = project(c * per_chunk + lane)
-        spans = [owner(variant, g) for g in range(groups)]
-        spans = [(start_ref[group], slot < count_ref[group]) for group in spans]
-
-        def picked(lane, g):
-            start, inside = spans[g]
-            return jnp.where(inside, rows_ref[lane, pl.ds(start, capacity), :], 0.0)
-
-        for lane in range(per_chunk):
-            ship(0, c, [(lane, g, picked(lane, g)) for g in range(groups // 2, groups)])
-        for copy in copies(0, c):
-            copy.start()
-        for lane in range(per_chunk):
-            held = [picked(lane, g) for g in range(groups // 2)]
-            for g, value in enumerate(held):
-                kept[c * per_chunk + lane, g] = value
+    def begin(first):
+        for lane in range(begin_chunks * per_chunk):
+            rows_ref[lane, :rows, :] = project(first * per_chunk + lane)
+        for k in range(begin_chunks):
+            c = first + k
+            spans = [owner(variant_of(c), g) for g in range(groups)]
+            spans = [(start_ref[group], slot < count_ref[group]) for group in spans]
+
+            def picked(lane, g):
+                start, inside = spans[g]
+                row = rows_ref[k * per_chunk + lane, pl.ds(start, capacity), :]
+                return jnp.where(inside, row, 0.0)
+
+            for lane in range(per_chunk):
+                ship(0, c, [(lane, g, picked(lane, g)) for g in range(groups // 2, groups)])
+            for copy in copies(0, c):
+                copy.start()
+            for lane in range(per_chunk):
+                held = [picked(lane, g) for g in range(groups // 2)]
+                for g, value in enumerate(held):
+                    kept[c * per_chunk + lane, g] = value
 
     def advance(stage, c):
         for copy in copies(stage - 1, c):
@@ -296,7 +320,7 @@
                 kept[c * per_chunk + lane, g] = tile
 
     def step_body(step, _):
-        @pl.when(step < chunks)
+        @pl.when((step < chunks) & (step % begin_chunks == 0))
         def _():
             begin(step)
 
@@ -329,10 +353,11 @@
 
     smem = pl.BlockSpec(memory_space=pltpu.SMEM)
     vmem = pl.BlockSpec(memory_space=pltpu.VMEM)
-    hbm = pl.BlockSpec(memory_space=pl.ANY)
+    hbm = pl.BlockSpec(memory_space=pltpu.HBM)
     dma = pltpu.SemaphoreType.DMA
     f32, bf16 = jnp.float32, jnp.bfloat16
-    plane = pltpu.VMEM((segments * (edge + pitch_extra), rows), f32)
+    together = math.gcd(angles, 2)
+    plane = pltpu.VMEM((together, segments * (edge + pitch_extra), rows), f32)
     halves = [groups >> (stage + 1) for stage in range(stages)]
     data = [pltpu.VMEM((chunks, per_chunk, half, capacity, edge), jnp.int16) for half in halves]
     unit = [pltpu.VMEM((chunks, per_chunk * half, edge), f32) for half in halves]
@@ -348,11 +373,11 @@
             pltpu.VMEM(powers.shape, f32),
             pltpu.VMEM(tiles.shape, bf16),
             plane, plane, plane,
-            pltpu.VMEM((2, segments, rows), f32),
+            pltpu.VMEM((together, 2, segments, rows), f32),
             pltpu.VMEM((angles, segments, rows, edge), bf16),
             pltpu.VMEM((cores - 1, angles, segments, rows, edge), bf16),
             pltpu.SMEM((groups,), jnp.int32),
-            pltpu.VMEM((per_chunk, rows + capacity, edge), f32),
+            pltpu.VMEM((math.gcd(chunks, 2) * per_chunk, rows + capacity, edge), f32),
             pltpu.VMEM((blocks, groups // 2, capacity, edge), f32),
             dma((angles,)),
             dma((4,)),

time: 47.7 us -> 48 us (level)
  no operation moved by 1% of the time
where the time goes in v5:
time: 48 us; the launch traced here: 47.7 us
  Pallas kernels  45.8 us (95%)
  local copies, waits for them, and re-layouts  1.87 us (4%)
    pallas_call x1, Pallas kernels, per_device(): pl.pallas_call(functools.partial(whole_kernel, stages, cores, chunks), ou...  45.8 us
    unnamed x1, local copies, waits for them, and re-layouts  1.87 us

profile of v5, /device:TPU:0, one launch (start us, length us, event | category | flops | bytes accessed | tf_op | source)
XLA Modules:
  0.0 47.7 jit_solution(15141479557714526838)
XLA Ops:
  0.0 45.8 %tomography.1 = f32[32,32,128]{2,1,0:T(8,128)} custom-call(s32[8]{0:T(128)} %count_ref.1, s32[64,64]{1,0:T(8,128)} %seg_ref.1, s32[64,64]{1,0:T(8,128)} %tile_ref.1, s32[64]{0:T(128)} %order_ref.1, f32[4,128,2048]{2,1,0:T(8,128)} %x_hbm.1, bf16[256,256]{1,0:T(8,128)(2,1)} %constant.6.clone.forward_hbm, bf16[256,256]{1,0:T(8,128)(2,1)} %constant.7.clone.inverse_hbm, ...), custom_call_target="tpu_custom_call" | custom-call | tf_op jit(solution)/shard_map/tomography/pallas_call | solution.py:364
  45.8 1.9 %copy.11 = f32[1,32,32,128]{3,2,1,0:T(8,128)} copy(f32[1,32,32,128]{3,2,1,0:T(8,128)} %bitcast.1) | data formatting | bytes 1048576

commit v6 on v4

--- a/solution.py
+++ b/solution.py
@@ -207,7 +207,7 @@
         )
 
     def variant_of(c):
-        return (c + 1) % 2 if stages > 1 else 0
+        return 1 - ((c + 2) % 4) // 3 if stages > 1 else 0
 
     def owner(variant, position):
         group = place
@@ -365,7 +365,7 @@
             *data, *data, *unit, *unit,
         ],
         compiler_params=pltpu.CompilerParams(
-            vmem_limit_bytes=60 * 2**20, collective_id=0, has_side_effects=True
+            vmem_limit_bytes=51 * 2**20, collective_id=0, has_side_effects=True
         ),
         name="tomography",
     )(

time: 47.7 us -> 55.7 us (1.17)
  local copies, waits for them, and re-layouts: 1.87 us -> 7.37 us
  Pallas kernels: 45.5 us -> 47.9 us
    unnamed x1 -> x17, local copies, waits for them, and re-layouts: 1.87 us -> 7.37 us
    pallas_call x1, Pallas kernels: 45.5 us -> 47.9 us  [per_device(): pl.pallas_call(functools.partial(whole_kernel, stages, cores, chunks), ou...]
where the time goes in v6:
time: 55.7 us; the launch traced here: 55.3 us
  Pallas kernels  47.9 us (86%)
  local copies, waits for them, and re-layouts  7.37 us (13%)
    pallas_call x1, Pallas kernels, per_device(): pl.pallas_call(functools.partial(whole_kernel, stages, cores, chunks), ou...  47.9 us
    unnamed x17, local copies, waits for them, and re-layouts  7.37 us

profile of v6, /device:TPU:0, one launch (start us, length us, event | category | flops | bytes accessed | tf_op | source)
XLA Modules:
  0.0 55.3 jit_solution(4143844324522678278)
XLA Ops:
  0.0 0.0 copy-start
  0.0 1.0 %copy-done = bf16[16,128,128]{2,1,0:T(8,128)(2,1)S(1)} copy-done((bf16[16,128,128]{2,1,0:T(8,128)(2,1)S(1)}, bf16[16,128,128]{2,1,0:T(8,128)(2,1)}, u32[]{:S(2)}) %copy-start) | copy-done | bytes 524312
  1.0 0.0 copy-start.1
  1.0 0.9 %copy-done.1 = f32[256,128]{1,0:T(8,128)S(1)} copy-done((f32[256,128]{1,0:T(8,128)S(1)}, f32[256,128]{1,0:T(8,128)}, u32[]{:S(2)}) %copy-start.1) | copy-done | bytes 131096
  1.9 0.0 copy-start.2
  1.9 0.9 %copy-done.2 = bf16[256,256]{1,0:T(8,128)(2,1)S(1)} copy-done((bf16[256,256]{1,0:T(8,128)(2,1)S(1)}, bf16[256,256]{1,0:T(8,128)(2,1)}, u32[]{:S(2)}) %copy-start.2) | copy-done | bytes 131096
  2.9 0.0 copy-start.3
  2.9 0.9 %copy-done.3 = bf16[256,256]{1,0:T(8,128)(2,1)S(1)} copy-done((bf16[256,256]{1,0:T(8,128)(2,1)S(1)}, bf16[256,256]{1,0:T(8,128)(2,1)}, u32[]{:S(2)}) %copy-start.3) | copy-done | bytes 131096
  3.8 0.0 copy-start.4
  3.8 0.8 %copy-done.4 = s32[64,64]{1,0:T(8,128)S(1)} copy-done((s32[64,64]{1,0:T(8,128)S(1)}, s32[64,64]{1,0:T(8,128)}, u32[]{:S(2)}) %copy-start.4) | copy-done | bytes 16408
  4.5 0.0 copy-start.5
  4.5 0.8 %copy-done.5 = s32[64,64]{1,0:T(8,128)S(1)} copy-done((s32[64,64]{1,0:T(8,128)S(1)}, s32[64,64]{1,0:T(8,128)}, u32[]{:S(2)}) %copy-start.5) | copy-done | bytes 16408
  5.3 0.0 copy-start.6
  5.3 0.7 %copy-done.6 = s32[8]{0:T(128)S(1)} copy-done((s32[8]{0:T(128)S(1)}, s32[8]{0:T(128)}, u32[]{:S(2)}) %copy-start.6) | copy-done | bytes 56
  5.9 0.0 copy-start.7
  5.9 0.7 %copy-done.7 = s32[64]{0:T(128)S(1)} copy-done((s32[64]{0:T(128)S(1)}, s32[64]{0:T(128)}, u32[]{:S(2)}) %copy-start.7) | copy-done | bytes 280
  6.6 47.9 %tomography.1 = f32[32,32,128]{2,1,0:T(8,128)S(1)} custom-call(s32[8]{0:T(128)S(1)} %copy-done.6, s32[64,64]{1,0:T(8,128)S(1)} %copy-done.4, s32[64,64]{1,0:T(8,128)S(1)} %copy-done.5, s32[64]{0:T(128)S(1)} %copy-done.7, f32[4,128,2048]{2,1,0:T(8,128)} %x_hbm.1, bf16[256,256]{1,0:T(8,128)(2,1)S(1)} %copy-done.3, bf16[256,256]{1,0:T(8,128)(2,1)S(1)} %copy-done.2, ...), custom_call_target="tpu_custom_call" | custom-call | tf_op jit(solution)/shard_map/tomography/pallas_call | solution.py:339
  54.5 0.8 %copy.11 = f32[1,32,32,128]{3,2,1,0:T(8,128)} copy(f32[1,32,32,128]{3,2,1,0:T(8,128)S(1)} %bitcast.1) | data formatting | bytes 1048576
Async XLA Ops:
  0.0 1.0 %copy-start = (bf16[16,128,128]{2,1,0:T(8,128)(2,1)S(1)}, bf16[16,128,128]{2,1,0:T(8,128)(2,1)}, u32[]{:S(2)}) copy-start(bf16[16,128,128]{2,1,0:T(8,128)(2,1)} %tiles_hbm.1) | copy-start | bytes 1572868
  1.0 0.9 %copy-start.1 = (f32[256,128]{1,0:T(8,128)S(1)}, f32[256,128]{1,0:T(8,128)}, u32[]{:S(2)}) copy-start(f32[256,128]{1,0:T(8,128)} %constant.8.clone.power_hbm) | copy-start | bytes 393220
  1.9 0.9 %copy-start.2 = (bf16[256,256]{1,0:T(8,128)(2,1)S(1)}, bf16[256,256]{1,0:T(8,128)(2,1)}, u32[]{:S(2)}) copy-start(bf16[256,256]{1,0:T(8,128)(2,1)} %constant.7.clone.inverse_hbm) | copy-start | bytes 393220
  2.9 0.9 %copy-start.3 = (bf16[256,256]{1,0:T(8,128)(2,1)S(1)}, bf16[256,256]{1,0:T(8,128)(2,1)}, u32[]{:S(2)}) copy-start(bf16[256,256]{1,0:T(8,128)(2,1)} %constant.6.clone.forward_hbm) | copy-start | bytes 393220
  3.8 0.8 %copy-start.4 = (s32[64,64]{1,0:T(8,128)S(1)}, s32[64,64]{1,0:T(8,128)}, u32[]{:S(2)}) copy-start(s32[64,64]{1,0:T(8,128)} %seg_ref.1) | copy-start | bytes 49156
  4.5 0.8 %copy-start.5 = (s32[64,64]{1,0:T(8,128)S(1)}, s32[64,64]{1,0:T(8,128)}, u32[]{:S(2)}) copy-start(s32[64,64]{1,0:T(8,128)} %tile_ref.1) | copy-start | bytes 49156
  5.3 0.7 %copy-start.6 = (s32[8]{0:T(128)S(1)}, s32[8]{0:T(128)}, u32[]{:S(2)}) copy-start(s32[8]{0:T(128)} %count_ref.1) | copy-start | bytes 100
  5.9 0.7 %copy-start.7 = (s32[64]{0:T(128)S(1)}, s32[64]{0:T(128)}, u32[]{:S(2)}) copy-start(s32[64]{0:T(128)} %order_ref.1) | copy-start | bytes 772

commit v7 on v4

--- a/solution.py
+++ b/solution.py
@@ -207,7 +207,7 @@
         )
 
     def variant_of(c):
-        return (c + 1) % 2 if stages > 1 else 0
+        return ((c + 2) % 4) // 3 if stages > 1 else 0
 
     def owner(variant, position):
         group = place

time: 47.7 us -> 49.3 us (1.034)
  Pallas kernels: 45.5 us -> 47.1 us
    pallas_call x1, Pallas kernels: 45.5 us -> 47.1 us  [per_device(): pl.pallas_call(functools.partial(whole_kernel, stages, cores, chunks), ou...]
where the time goes in v7:
time: 49.3 us; the launch traced here: 49 us
  Pallas kernels  47.1 us (96%)
  local copies, waits for them, and re-layouts  1.87 us (4%)
    pallas_call x1, Pallas kernels, per_device(): pl.pallas_call(functools.partial(whole_kernel, stages, cores, chunks), ou...  47.1 us
    unnamed x1, local copies, waits for them, and re-layouts  1.87 us

profile of v7, /device:TPU:0, one launch (start us, length us, event | category | flops | bytes accessed | tf_op | source)
XLA Modules:
  0.0 49.0 jit_solution(6670461771875434335)
XLA Ops:
  0.0 47.1 %tomography.1 = f32[32,32,128]{2,1,0:T(8,128)} custom-call(s32[8]{0:T(128)} %count_ref.1, s32[64,64]{1,0:T(8,128)} %seg_ref.1, s32[64,64]{1,0:T(8,128)} %tile_ref.1, s32[64]{0:T(128)} %order_ref.1, f32[4,128,2048]{2,1,0:T(8,128)} %x_hbm.1, bf16[256,256]{1,0:T(8,128)(2,1)} %constant.6.clone.forward_hbm, bf16[256,256]{1,0:T(8,128)(2,1)} %constant.7.clone.inverse_hbm, ...), custom_call_target="tpu_custom_call" | custom-call | tf_op jit(solution)/shard_map/tomography/pallas_call | solution.py:339
  47.1 1.9 %copy.11 = f32[1,32,32,128]{3,2,1,0:T(8,128)} copy(f32[1,32,32,128]{3,2,1,0:T(8,128)} %bitcast.1) | data formatting | bytes 1048576
